TPU v7x, 512 devices: a whole 4x4x16 slice. The times are simulated.
512 devices in a mesh: ctx: 64 (over z_lo, x, y), tp: 8 (over z_hi, core).
Axes of the slice: x: 4, y: 4, z: 16 (z_hi: 4, z_lo: 4; z = z_hi * 4 + z_lo), core: 2. Of those that a mesh axis runs over, the one named last changes fastest.
Arguments:
- queries: bfloat16 [8192, 32, 128], P('ctx', 'tp'), may hold values from -16.25 to 16.25
- keys: bfloat16 [8192, 8, 128], P('ctx', 'tp'), may hold values from -4 to 4
- values: bfloat16 [8192, 8, 128], P('ctx', 'tp'), may hold values from -6 to 6
- grad_out: bfloat16 [8192, 32, 128], P('ctx', 'tp'), may hold values from -6 to 6
- saved_stats: float32 [2, 32, 8192], P(None, 'tp', 'ctx'), may hold values from -4608 to 4608, as said below
- positions: int32 [8192], P('ctx'), may hold values from 0 to 8191, as said below
Outputs:
- grad_queries: bfloat16 [8192, 32, 128], P('ctx', 'tp')
- grad_keys: bfloat16 [8192, 8, 128], P('ctx', 'tp')
- grad_values: bfloat16 [8192, 8, 128], P('ctx', 'tp')
Inputs may be any that keep to these rules, and one draw needn't show every extreme that they name: positions holds every number of 0 to 8191 once. It is made of 128 runs of 64 consecutive rising values: for d from 0 to 63, rows d * 128 to d * 128 + 63 hold the run starting at p(d) * 64, and the next 64 rows the run starting at (127 - p(d)) * 64, where p is a permutation of 0 to 63. saved_stats holds the forward pass's statistics for these queries, keys, values, grad_out and positions.
All inputs are finite; a program needn't handle non-finite values.
Results may differ from a plain program's by a relative error of at most 0.0075.
Values may be sent and summed in bfloat16 or wider, within the bound.
A program may use at most 64 MiB of HBM per device.

v0:
```python
import math

import jax
import jax.numpy as jnp
from jax import lax
from jax.sharding import PartitionSpec as P

masked_score = -1e30


def shifted(array, axis, by):
    length = lax.axis_size(axis)
    return lax.ppermute(array, axis, [(i, (i + by) % length) for i in range(length)])


def split_rows(values_in, heads_kv, half_rows):
    rows_dev, heads_q, head_dim = values_in.shape
    group_size = heads_q // heads_kv
    arranged = values_in.reshape(rows_dev, heads_kv, group_size, head_dim).transpose(1, 2, 0, 3)
    early_rows = arranged[:, :, :half_rows].reshape(heads_kv, group_size * half_rows, head_dim)
    late_rows = arranged[:, :, half_rows:].reshape(heads_kv, group_size * half_rows, head_dim)
    return (early_rows, late_rows)


def join_rows(early_rows, late_rows, group_size):
    heads_kv, rows_half, head_dim = early_rows.shape
    half_rows = rows_half // group_size
    combined = jnp.concatenate(
        [
            early_rows.reshape(heads_kv, group_size, half_rows, head_dim),
            late_rows.reshape(heads_kv, group_size, half_rows, head_dim),
        ],
        axis=2,
    )
    return combined.transpose(2, 0, 1, 3).reshape(2 * half_rows, heads_kv * group_size, head_dim)


def backward_tile(
    query_rows,
    grad_rows,
    query_pos,
    key_rows,
    value_rows,
    key_pos,
    log_total,
    row_delta,
    softmax_scale,
):
    scores = (
        jnp.einsum("bhkd,bhrd->bhkr", key_rows, query_rows, preferred_element_type=jnp.float32)
        * softmax_scale
    )
    visible = (key_pos[:, :, None] <= query_pos[:, None, :])[:, None]
    probs = jnp.exp(jnp.where(visible, scores - log_total[:, :, None, :], masked_score))
    grad_probs = jnp.einsum(
        "bhkd,bhrd->bhkr", value_rows, grad_rows, preferred_element_type=jnp.float32
    )
    grad_scores = (probs * (grad_probs - row_delta[:, :, None, :])).astype(jnp.bfloat16)
    grad_value_part = jnp.einsum(
        "bhkr,bhrd->bhkd", probs.astype(jnp.bfloat16), grad_rows, preferred_element_type=jnp.float32
    )
    grad_key_part = jnp.einsum(
        "bhkr,bhrd->bhkd", grad_scores, query_rows, preferred_element_type=jnp.float32
    )
    grad_query_part = jnp.einsum(
        "bhkr,bhkd->bhrd", grad_scores, key_rows, preferred_element_type=jnp.float32
    )
    return (grad_key_part, grad_value_part, grad_query_part)


def body(queries, keys, values, grad_out, saved_stats, positions):
    cycle_size = lax.axis_size("ctx")
    my_index = lax.axis_index("ctx")
    rows_dev, heads_kv, head_dim = keys.shape
    group_size = queries.shape[1] // heads_kv
    half_rows = rows_dev // 2
    softmax_scale = 1.0 / math.sqrt(head_dim)
    every_pos = lax.all_gather(positions, "ctx", axis=0, tiled=True)
    own_block = jnp.stack([keys, values]).transpose(0, 2, 1, 3)
    query_early, query_late = split_rows(queries, heads_kv, half_rows)
    grad_early, grad_late = split_rows(grad_out, heads_kv, half_rows)
    pos_early = jnp.tile(positions[:half_rows], group_size)
    pos_late = jnp.tile(positions[half_rows:], group_size)
    arranged_stats = saved_stats.reshape(2, heads_kv, group_size, rows_dev)
    stats_early = arranged_stats[:, :, :, :half_rows].reshape(2, heads_kv, group_size * half_rows)
    stats_late = arranged_stats[:, :, :, half_rows:].reshape(2, heads_kv, group_size * half_rows)
    log_early, delta_early = (stats_early[0], stats_early[1])
    log_late, delta_late = (stats_late[0], stats_late[1])

    def key_positions(source):
        return lax.dynamic_slice_in_dim(every_pos, source * rows_dev, rows_dev)

    def fetch_forward(kv_block, source):
        source = (source - 1) % cycle_size
        kv_block = shifted(kv_block, "ctx", 1)
        return (kv_block, source)

    def pass_forward(accumulated):
        return shifted(accumulated, "ctx", 1)

    def pair_inputs(kv_block, key_pos):
        lowered = key_pos[0] <= positions[0]
        block_early = kv_block[:, :, :half_rows]
        block_late = kv_block[:, :, half_rows:]
        pair_keys = jnp.stack([block_early, jnp.where(lowered, block_early, block_late)])
        pair_pos = jnp.stack(
            [key_pos[:half_rows], jnp.where(lowered, key_pos[:half_rows], key_pos[half_rows:])]
        )
        pair_query = jnp.stack([query_late, jnp.where(lowered, query_early, query_late)])
        pair_grad = jnp.stack([grad_late, jnp.where(lowered, grad_early, grad_late)])
        pair_query_pos = jnp.stack([pos_late, jnp.where(lowered, pos_early, pos_late)])
        return (lowered, pair_keys, pair_pos, pair_query, pair_grad, pair_query_pos)

    def absorb_grads(kv_block, key_pos, accumulated, query_grads):
        lowered, pair_keys, pair_pos, pair_query, pair_grad, pair_query_pos = pair_inputs(
            kv_block, key_pos
        )
        pair_log = jnp.stack([log_late, jnp.where(lowered, log_early, log_late)])
        pair_delta = jnp.stack([delta_late, jnp.where(lowered, delta_early, delta_late)])
        grad_key_part, grad_value_part, grad_query_part = backward_tile(
            pair_query,
            pair_grad,
            pair_query_pos,
            pair_keys[:, 0],
            pair_keys[:, 1],
            pair_pos,
            pair_log,
            pair_delta,
            softmax_scale,
        )
        grad_q_early, grad_q_late = query_grads
        grad_q_late = grad_q_late + grad_query_part[0] + jnp.where(lowered, 0.0, grad_query_part[1])
        grad_q_early = grad_q_early + jnp.where(lowered, grad_query_part[1], 0.0)
        first_pair = jnp.stack([grad_key_part[0], grad_value_part[0]])
        second_pair = jnp.stack([grad_key_part[1], grad_value_part[1]])
        accumulated = accumulated + jnp.concatenate(
            [
                first_pair + jnp.where(lowered, second_pair, 0.0),
                jnp.where(lowered, 0.0, second_pair),
            ],
            axis=2,
        )
        return (accumulated, (grad_q_early, grad_q_late))

    zero_accum = jnp.zeros((2, heads_kv, rows_dev, head_dim), jnp.float32)
    zero_query = jnp.zeros((heads_kv, group_size * half_rows, head_dim), jnp.float32)
    own_accum, query_grads = absorb_grads(
        own_block, positions, zero_accum, (zero_query, zero_query)
    )
    extra_key, extra_value, extra_query = backward_tile(
        query_late[None],
        grad_late[None],
        pos_late[None],
        own_block[None, 0, :, half_rows:],
        own_block[None, 1, :, half_rows:],
        positions[None, half_rows:],
        log_late[None],
        delta_late[None],
        softmax_scale,
    )
    own_accum = own_accum.at[:, :, half_rows:].add(jnp.stack([extra_key[0], extra_value[0]]))
    query_grads = (query_grads[0], query_grads[1] + extra_query[0])
    kv_block, source = fetch_forward(own_block, my_index)
    accumulated, query_grads = absorb_grads(
        kv_block, key_positions(source), zero_accum, query_grads
    )

    def backward_turn(turn_index, carried):
        kv_block, source, accumulated, query_grads = carried
        for inner_step in range(2):
            kv_block, source = fetch_forward(kv_block, source)
            accumulated = pass_forward(accumulated)
            accumulated, query_grads = absorb_grads(
                kv_block, key_positions(source), accumulated, query_grads
            )
        return (kv_block, source, accumulated, query_grads)

    kv_block, source, accumulated, query_grads = lax.fori_loop(
        0, (cycle_size - 2) // 2, backward_turn, (kv_block, source, accumulated, query_grads)
    )
    key_grads = pass_forward(accumulated) + own_accum
    grad_queries = (join_rows(query_grads[0], query_grads[1], group_size) * softmax_scale).astype(
        jnp.bfloat16
    )
    grad_keys = (key_grads[0] * softmax_scale).transpose(1, 0, 2).astype(jnp.bfloat16)
    grad_values = key_grads[1].transpose(1, 0, 2).astype(jnp.bfloat16)
    return (grad_queries, grad_keys, grad_values)


def solution(mesh):
    in_specs = (
        P("ctx", "tp", None),
        P("ctx", "tp", None),
        P("ctx", "tp", None),
        P("ctx", "tp", None),
        P(None, "tp", "ctx"),
        P("ctx"),
    )
    out_specs = (P("ctx", "tp", None), P("ctx", "tp", None), P("ctx", "tp", None))
    return jax.shard_map(body, mesh=mesh, in_specs=in_specs, out_specs=out_specs, check_vma=False)
```

profile of v0, /device:TPU:128, one launch (start us, length us, event | category | flops | bytes accessed | tf_op | source)
XLA Modules:
  0.0 1435.9 jit_solution(16560855712067649852)
XLA Ops:
  6.8 185.5 %all-gather = s32[64,1,128]{2,1,0:T(1,128)S(1)} all-gather(s32[1,1,128]{2,1,0:T(1,128)S(1)} %bitcast.391), channel_id=1, replica_groups=mesh['ctx'=64,'tp'=8] {'ctx'}, dimensions={0}, use_global_device_ids=true | all-gather | bytes 33280 | tf_op jit(solution)/shard_map/all_gather | solution.py:78
  196.4 1225.3 %while.24 = (s32[]{:T(128)}, bf16[2,1,128,128]{3,2,0,1:T(8,128)(2,1)S(1)}, s32[]{:T(128)}, f32[2,1,128,128]{3,2,0,1:T(8,128)S(1)}, f32[1,256,128]{2,1,0:T(8,128)...) while((s32[]{:T(128)}, ...), condition=%wide.region_1.2_spmd.clone.clone, body=%wide.region_0.1_spmd.clone.clone.sunk | while | flops 85824416 | bytes 8713493 | solution.py:178
  224.9 10.8 collective-permute-done.3
  264.1 11.2 collective-permute-done.3
  304.3 10.8 collective-permute-done.3
  343.6 10.8 collective-permute-done.3
  382.9 10.8 collective-permute-done.3
  422.1 11.5 collective-permute-done.3
  462.3 11.3 collective-permute-done.3
  502.0 10.8 collective-permute-done.3
  541.3 10.8 collective-permute-done.3
  581.0 10.8 collective-permute-done.3
  620.5 10.8 collective-permute-done.3
  659.7 10.8 collective-permute-done.3
  699.0 11.2 collective-permute-done.3
  739.2 10.8 collective-permute-done.3
  778.5 10.8 collective-permute-done.3
  817.7 10.8 collective-permute-done.3
  857.0 11.5 collective-permute-done.3
  897.1 11.3 collective-permute-done.3
  936.9 10.8 collective-permute-done.3
  976.1 10.8 collective-permute-done.3
  1015.9 10.8 collective-permute-done.3
  1055.3 10.8 collective-permute-done.3
  1094.6 10.8 collective-permute-done.3
  1133.8 11.2 collective-permute-done.3
  1174.0 10.8 collective-permute-done.3
  1213.3 10.8 collective-permute-done.3
  1252.6 10.8 collective-permute-done.3
  1291.8 12.1 collective-permute-done.3
  1332.4 10.8 collective-permute-done.3
  1371.7 10.8 collective-permute-done.3
  (1408 shorter events, 910.1 us)
Async XLA Ops:
  1.4 193.8 %collective-permute-start.4 = (bf16[2,1,128,128]{3,2,0,1:T(8,128)(2,1)S(1)}, bf16[2,1,128,128]{3,2,0,1:T(8,128)(2,1)S(1)}, u32[]{:S(2)}, u32[]{:S(2)}) collective-permute-start(bf16[2,1,128,128]{3,2,0,1:T(8,128)(2,1)S(1)} %maximum_bitcast_fusion.6), channel_id=1, source_target_pairs={{0,8},{8,16},{16,24},{24,32},{32,40},{40,48},{48,56},{56,64},{64,7... | collective-permute-start | bytes 196616 | tf_op jit(solution)/shard_map/ppermute | solution.py:13
  198.4 24.4 %collective-permute-start.2 = (f32[2,1,128,128]{3,2,0,1:T(8,128)S(1)}, f32[2,1,128,128]{3,2,0,1:T(8,128)S(1)}, u32[]{:S(2)}, u32[]{:S(2)}) collective-permute-start(f32[2,1,128,128]{3,2,0,1:T(8,128)S(1)} %get-tuple-element.838), channel_id=1, source_target_pairs={{0,8},{8,16},{16,24},{24,32},{32,40},{40,48},{48,56},{56,64},{64,7... | collective-permute-start | bytes 393224 | tf_op jit(solution)/shard_map/while/body/eval_jaxpr/ppermute | solution.py:13
  237.6 24.4 %collective-permute-start.2 = (f32[2,1,128,128]{3,2,0,1:T(8,128)S(1)}, f32[2,1,128,128]{3,2,0,1:T(8,128)S(1)}, u32[]{:S(2)}, u32[]{:S(2)}) collective-permute-start(f32[2,1,128,128]{3,2,0,1:T(8,128)S(1)} %get-tuple-element.838), channel_id=1, source_target_pairs={{0,8},{8,16},{16,24},{24,32},{32,40},{40,48},{48,56},{56,64},{64,7... | collective-permute-start | bytes 393224 | tf_op jit(solution)/shard_map/while/body/eval_jaxpr/ppermute | solution.py:13
  277.2 25.0 %collective-permute-start.2 = (f32[2,1,128,128]{3,2,0,1:T(8,128)S(1)}, f32[2,1,128,128]{3,2,0,1:T(8,128)S(1)}, u32[]{:S(2)}, u32[]{:S(2)}) collective-permute-start(f32[2,1,128,128]{3,2,0,1:T(8,128)S(1)} %get-tuple-element.838), channel_id=1, source_target_pairs={{0,8},{8,16},{16,24},{24,32},{32,40},{40,48},{48,56},{56,64},{64,7... | collective-permute-start | bytes 393224 | tf_op jit(solution)/shard_map/while/body/eval_jaxpr/ppermute | solution.py:13
  317.1 24.4 %collective-permute-start.2 = (f32[2,1,128,128]{3,2,0,1:T(8,128)S(1)}, f32[2,1,128,128]{3,2,0,1:T(8,128)S(1)}, u32[]{:S(2)}, u32[]{:S(2)}) collective-permute-start(f32[2,1,128,128]{3,2,0,1:T(8,128)S(1)} %get-tuple-element.838), channel_id=1, source_target_pairs={{0,8},{8,16},{16,24},{24,32},{32,40},{40,48},{48,56},{56,64},{64,7... | collective-permute-start | bytes 393224 | tf_op jit(solution)/shard_map/while/body/eval_jaxpr/ppermute | solution.py:13
  356.4 24.4 %collective-permute-start.2 = (f32[2,1,128,128]{3,2,0,1:T(8,128)S(1)}, f32[2,1,128,128]{3,2,0,1:T(8,128)S(1)}, u32[]{:S(2)}, u32[]{:S(2)}) collective-permute-start(f32[2,1,128,128]{3,2,0,1:T(8,128)S(1)} %get-tuple-element.838), channel_id=1, source_target_pairs={{0,8},{8,16},{16,24},{24,32},{32,40},{40,48},{48,56},{56,64},{64,7... | collective-permute-start | bytes 393224 | tf_op jit(solution)/shard_map/while/body/eval_jaxpr/ppermute | solution.py:13
  395.6 24.4 %collective-permute-start.2 = (f32[2,1,128,128]{3,2,0,1:T(8,128)S(1)}, f32[2,1,128,128]{3,2,0,1:T(8,128)S(1)}, u32[]{:S(2)}, u32[]{:S(2)}) collective-permute-start(f32[2,1,128,128]{3,2,0,1:T(8,128)S(1)} %get-tuple-element.838), channel_id=1, source_target_pairs={{0,8},{8,16},{16,24},{24,32},{32,40},{40,48},{48,56},{56,64},{64,7... | collective-permute-start | bytes 393224 | tf_op jit(solution)/shard_map/while/body/eval_jaxpr/ppermute | solution.py:13
  435.6 24.5 %collective-permute-start.2 = (f32[2,1,128,128]{3,2,0,1:T(8,128)S(1)}, f32[2,1,128,128]{3,2,0,1:T(8,128)S(1)}, u32[]{:S(2)}, u32[]{:S(2)}) collective-permute-start(f32[2,1,128,128]{3,2,0,1:T(8,128)S(1)} %get-tuple-element.838), channel_id=1, source_target_pairs={{0,8},{8,16},{16,24},{24,32},{32,40},{40,48},{48,56},{56,64},{64,7... | collective-permute-start | bytes 393224 | tf_op jit(solution)/shard_map/while/body/eval_jaxpr/ppermute | solution.py:13
  475.5 24.4 %collective-permute-start.2 = (f32[2,1,128,128]{3,2,0,1:T(8,128)S(1)}, f32[2,1,128,128]{3,2,0,1:T(8,128)S(1)}, u32[]{:S(2)}, u32[]{:S(2)}) collective-permute-start(f32[2,1,128,128]{3,2,0,1:T(8,128)S(1)} %get-tuple-element.838), channel_id=1, source_target_pairs={{0,8},{8,16},{16,24},{24,32},{32,40},{40,48},{48,56},{56,64},{64,7... | collective-permute-start | bytes 393224 | tf_op jit(solution)/shard_map/while/body/eval_jaxpr/ppermute | solution.py:13
  514.8 24.4 %collective-permute-start.2 = (f32[2,1,128,128]{3,2,0,1:T(8,128)S(1)}, f32[2,1,128,128]{3,2,0,1:T(8,128)S(1)}, u32[]{:S(2)}, u32[]{:S(2)}) collective-permute-start(f32[2,1,128,128]{3,2,0,1:T(8,128)S(1)} %get-tuple-element.838), channel_id=1, source_target_pairs={{0,8},{8,16},{16,24},{24,32},{32,40},{40,48},{48,56},{56,64},{64,7... | collective-permute-start | bytes 393224 | tf_op jit(solution)/shard_map/while/body/eval_jaxpr/ppermute | solution.py:13
  554.0 24.9 %collective-permute-start.2 = (f32[2,1,128,128]{3,2,0,1:T(8,128)S(1)}, f32[2,1,128,128]{3,2,0,1:T(8,128)S(1)}, u32[]{:S(2)}, u32[]{:S(2)}) collective-permute-start(f32[2,1,128,128]{3,2,0,1:T(8,128)S(1)} %get-tuple-element.838), channel_id=1, source_target_pairs={{0,8},{8,16},{16,24},{24,32},{32,40},{40,48},{48,56},{56,64},{64,7... | collective-permute-start | bytes 393224 | tf_op jit(solution)/shard_map/while/body/eval_jaxpr/ppermute | solution.py:13
  593.8 24.6 %collective-permute-start.2 = (f32[2,1,128,128]{3,2,0,1:T(8,128)S(1)}, f32[2,1,128,128]{3,2,0,1:T(8,128)S(1)}, u32[]{:S(2)}, u32[]{:S(2)}) collective-permute-start(f32[2,1,128,128]{3,2,0,1:T(8,128)S(1)} %get-tuple-element.838), channel_id=1, source_target_pairs={{0,8},{8,16},{16,24},{24,32},{32,40},{40,48},{48,56},{56,64},{64,7... | collective-permute-start | bytes 393224 | tf_op jit(solution)/shard_map/while/body/eval_jaxpr/ppermute | solution.py:13
  633.2 24.4 %collective-permute-start.2 = (f32[2,1,128,128]{3,2,0,1:T(8,128)S(1)}, f32[2,1,128,128]{3,2,0,1:T(8,128)S(1)}, u32[]{:S(2)}, u32[]{:S(2)}) collective-permute-start(f32[2,1,128,128]{3,2,0,1:T(8,128)S(1)} %get-tuple-element.838), channel_id=1, source_target_pairs={{0,8},{8,16},{16,24},{24,32},{32,40},{40,48},{48,56},{56,64},{64,7... | collective-permute-start | bytes 393224 | tf_op jit(solution)/shard_map/while/body/eval_jaxpr/ppermute | solution.py:13
  672.5 24.4 %collective-permute-start.2 = (f32[2,1,128,128]{3,2,0,1:T(8,128)S(1)}, f32[2,1,128,128]{3,2,0,1:T(8,128)S(1)}, u32[]{:S(2)}, u32[]{:S(2)}) collective-permute-start(f32[2,1,128,128]{3,2,0,1:T(8,128)S(1)} %get-tuple-element.838), channel_id=1, source_target_pairs={{0,8},{8,16},{16,24},{24,32},{32,40},{40,48},{48,56},{56,64},{64,7... | collective-permute-start | bytes 393224 | tf_op jit(solution)/shard_map/while/body/eval_jaxpr/ppermute | solution.py:13
  712.1 25.0 %collective-permute-start.2 = (f32[2,1,128,128]{3,2,0,1:T(8,128)S(1)}, f32[2,1,128,128]{3,2,0,1:T(8,128)S(1)}, u32[]{:S(2)}, u32[]{:S(2)}) collective-permute-start(f32[2,1,128,128]{3,2,0,1:T(8,128)S(1)} %get-tuple-element.838), channel_id=1, source_target_pairs={{0,8},{8,16},{16,24},{24,32},{32,40},{40,48},{48,56},{56,64},{64,7... | collective-permute-start | bytes 393224 | tf_op jit(solution)/shard_map/while/body/eval_jaxpr/ppermute | solution.py:13
  751.9 24.4 %collective-permute-start.2 = (f32[2,1,128,128]{3,2,0,1:T(8,128)S(1)}, f32[2,1,128,128]{3,2,0,1:T(8,128)S(1)}, u32[]{:S(2)}, u32[]{:S(2)}) collective-permute-start(f32[2,1,128,128]{3,2,0,1:T(8,128)S(1)} %get-tuple-element.838), channel_id=1, source_target_pairs={{0,8},{8,16},{16,24},{24,32},{32,40},{40,48},{48,56},{56,64},{64,7... | collective-permute-start | bytes 393224 | tf_op jit(solution)/shard_map/while/body/eval_jaxpr/ppermute | solution.py:13
  791.2 24.4 %collective-permute-start.2 = (f32[2,1,128,128]{3,2,0,1:T(8,128)S(1)}, f32[2,1,128,128]{3,2,0,1:T(8,128)S(1)}, u32[]{:S(2)}, u32[]{:S(2)}) collective-permute-start(f32[2,1,128,128]{3,2,0,1:T(8,128)S(1)} %get-tuple-element.838), channel_id=1, source_target_pairs={{0,8},{8,16},{16,24},{24,32},{32,40},{40,48},{48,56},{56,64},{64,7... | collective-permute-start | bytes 393224 | tf_op jit(solution)/shard_map/while/body/eval_jaxpr/ppermute | solution.py:13
  830.5 24.4 %collective-permute-start.2 = (f32[2,1,128,128]{3,2,0,1:T(8,128)S(1)}, f32[2,1,128,128]{3,2,0,1:T(8,128)S(1)}, u32[]{:S(2)}, u32[]{:S(2)}) collective-permute-start(f32[2,1,128,128]{3,2,0,1:T(8,128)S(1)} %get-tuple-element.838), channel_id=1, source_target_pairs={{0,8},{8,16},{16,24},{24,32},{32,40},{40,48},{48,56},{56,64},{64,7... | collective-permute-start | bytes 393224 | tf_op jit(solution)/shard_map/while/body/eval_jaxpr/ppermute | solution.py:13
  870.5 24.5 %collective-permute-start.2 = (f32[2,1,128,128]{3,2,0,1:T(8,128)S(1)}, f32[2,1,128,128]{3,2,0,1:T(8,128)S(1)}, u32[]{:S(2)}, u32[]{:S(2)}) collective-permute-start(f32[2,1,128,128]{3,2,0,1:T(8,128)S(1)} %get-tuple-element.838), channel_id=1, source_target_pairs={{0,8},{8,16},{16,24},{24,32},{32,40},{40,48},{48,56},{56,64},{64,7... | collective-permute-start | bytes 393224 | tf_op jit(solution)/shard_map/while/body/eval_jaxpr/ppermute | solution.py:13
  910.4 24.4 %collective-permute-start.2 = (f32[2,1,128,128]{3,2,0,1:T(8,128)S(1)}, f32[2,1,128,128]{3,2,0,1:T(8,128)S(1)}, u32[]{:S(2)}, u32[]{:S(2)}) collective-permute-start(f32[2,1,128,128]{3,2,0,1:T(8,128)S(1)} %get-tuple-element.838), channel_id=1, source_target_pairs={{0,8},{8,16},{16,24},{24,32},{32,40},{40,48},{48,56},{56,64},{64,7... | collective-permute-start | bytes 393224 | tf_op jit(solution)/shard_map/while/body/eval_jaxpr/ppermute | solution.py:13
  949.6 24.4 %collective-permute-start.2 = (f32[2,1,128,128]{3,2,0,1:T(8,128)S(1)}, f32[2,1,128,128]{3,2,0,1:T(8,128)S(1)}, u32[]{:S(2)}, u32[]{:S(2)}) collective-permute-start(f32[2,1,128,128]{3,2,0,1:T(8,128)S(1)} %get-tuple-element.838), channel_id=1, source_target_pairs={{0,8},{8,16},{16,24},{24,32},{32,40},{40,48},{48,56},{56,64},{64,7... | collective-permute-start | bytes 393224 | tf_op jit(solution)/shard_map/while/body/eval_jaxpr/ppermute | solution.py:13
  988.9 24.9 %collective-permute-start.2 = (f32[2,1,128,128]{3,2,0,1:T(8,128)S(1)}, f32[2,1,128,128]{3,2,0,1:T(8,128)S(1)}, u32[]{:S(2)}, u32[]{:S(2)}) collective-permute-start(f32[2,1,128,128]{3,2,0,1:T(8,128)S(1)} %get-tuple-element.838), channel_id=1, source_target_pairs={{0,8},{8,16},{16,24},{24,32},{32,40},{40,48},{48,56},{56,64},{64,7... | collective-permute-start | bytes 393224 | tf_op jit(solution)/shard_map/while/body/eval_jaxpr/ppermute | solution.py:13
  1028.6 24.6 %collective-permute-start.2 = (f32[2,1,128,128]{3,2,0,1:T(8,128)S(1)}, f32[2,1,128,128]{3,2,0,1:T(8,128)S(1)}, u32[]{:S(2)}, u32[]{:S(2)}) collective-permute-start(f32[2,1,128,128]{3,2,0,1:T(8,128)S(1)} %get-tuple-element.838), channel_id=1, source_target_pairs={{0,8},{8,16},{16,24},{24,32},{32,40},{40,48},{48,56},{56,64},{64,7... | collective-permute-start | bytes 393224 | tf_op jit(solution)/shard_map/while/body/eval_jaxpr/ppermute | solution.py:13
  1068.1 24.4 %collective-permute-start.2 = (f32[2,1,128,128]{3,2,0,1:T(8,128)S(1)}, f32[2,1,128,128]{3,2,0,1:T(8,128)S(1)}, u32[]{:S(2)}, u32[]{:S(2)}) collective-permute-start(f32[2,1,128,128]{3,2,0,1:T(8,128)S(1)} %get-tuple-element.838), channel_id=1, source_target_pairs={{0,8},{8,16},{16,24},{24,32},{32,40},{40,48},{48,56},{56,64},{64,7... | collective-permute-start | bytes 393224 | tf_op jit(solution)/shard_map/while/body/eval_jaxpr/ppermute | solution.py:13
  1107.3 24.4 %collective-permute-start.2 = (f32[2,1,128,128]{3,2,0,1:T(8,128)S(1)}, f32[2,1,128,128]{3,2,0,1:T(8,128)S(1)}, u32[]{:S(2)}, u32[]{:S(2)}) collective-permute-start(f32[2,1,128,128]{3,2,0,1:T(8,128)S(1)} %get-tuple-element.838), channel_id=1, source_target_pairs={{0,8},{8,16},{16,24},{24,32},{32,40},{40,48},{48,56},{56,64},{64,7... | collective-permute-start | bytes 393224 | tf_op jit(solution)/shard_map/while/body/eval_jaxpr/ppermute | solution.py:13
  1146.9 25.0 %collective-permute-start.2 = (f32[2,1,128,128]{3,2,0,1:T(8,128)S(1)}, f32[2,1,128,128]{3,2,0,1:T(8,128)S(1)}, u32[]{:S(2)}, u32[]{:S(2)}) collective-permute-start(f32[2,1,128,128]{3,2,0,1:T(8,128)S(1)} %get-tuple-element.838), channel_id=1, source_target_pairs={{0,8},{8,16},{16,24},{24,32},{32,40},{40,48},{48,56},{56,64},{64,7... | collective-permute-start | bytes 393224 | tf_op jit(solution)/shard_map/while/body/eval_jaxpr/ppermute | solution.py:13
  1186.8 24.4 %collective-permute-start.2 = (f32[2,1,128,128]{3,2,0,1:T(8,128)S(1)}, f32[2,1,128,128]{3,2,0,1:T(8,128)S(1)}, u32[]{:S(2)}, u32[]{:S(2)}) collective-permute-start(f32[2,1,128,128]{3,2,0,1:T(8,128)S(1)} %get-tuple-element.838), channel_id=1, source_target_pairs={{0,8},{8,16},{16,24},{24,32},{32,40},{40,48},{48,56},{56,64},{64,7... | collective-permute-start | bytes 393224 | tf_op jit(solution)/shard_map/while/body/eval_jaxpr/ppermute | solution.py:13
  1226.1 24.4 %collective-permute-start.2 = (f32[2,1,128,128]{3,2,0,1:T(8,128)S(1)}, f32[2,1,128,128]{3,2,0,1:T(8,128)S(1)}, u32[]{:S(2)}, u32[]{:S(2)}) collective-permute-start(f32[2,1,128,128]{3,2,0,1:T(8,128)S(1)} %get-tuple-element.838), channel_id=1, source_target_pairs={{0,8},{8,16},{16,24},{24,32},{32,40},{40,48},{48,56},{56,64},{64,7... | collective-permute-start | bytes 393224 | tf_op jit(solution)/shard_map/while/body/eval_jaxpr/ppermute | solution.py:13
  1265.3 24.4 %collective-permute-start.2 = (f32[2,1,128,128]{3,2,0,1:T(8,128)S(1)}, f32[2,1,128,128]{3,2,0,1:T(8,128)S(1)}, u32[]{:S(2)}, u32[]{:S(2)}) collective-permute-start(f32[2,1,128,128]{3,2,0,1:T(8,128)S(1)} %get-tuple-element.838), channel_id=1, source_target_pairs={{0,8},{8,16},{16,24},{24,32},{32,40},{40,48},{48,56},{56,64},{64,7... | collective-permute-start | bytes 393224 | tf_op jit(solution)/shard_map/while/body/eval_jaxpr/ppermute | solution.py:13
  1305.9 24.4 %collective-permute-start.2 = (f32[2,1,128,128]{3,2,0,1:T(8,128)S(1)}, f32[2,1,128,128]{3,2,0,1:T(8,128)S(1)}, u32[]{:S(2)}, u32[]{:S(2)}) collective-permute-start(f32[2,1,128,128]{3,2,0,1:T(8,128)S(1)} %get-tuple-element.838), channel_id=1, source_target_pairs={{0,8},{8,16},{16,24},{24,32},{32,40},{40,48},{48,56},{56,64},{64,7... | collective-permute-start | bytes 393224 | tf_op jit(solution)/shard_map/while/body/eval_jaxpr/ppermute | solution.py:13
  1345.2 24.4 %collective-permute-start.2 = (f32[2,1,128,128]{3,2,0,1:T(8,128)S(1)}, f32[2,1,128,128]{3,2,0,1:T(8,128)S(1)}, u32[]{:S(2)}, u32[]{:S(2)}) collective-permute-start(f32[2,1,128,128]{3,2,0,1:T(8,128)S(1)} %get-tuple-element.838), channel_id=1, source_target_pairs={{0,8},{8,16},{16,24},{24,32},{32,40},{40,48},{48,56},{56,64},{64,7... | collective-permute-start | bytes 393224 | tf_op jit(solution)/shard_map/while/body/eval_jaxpr/ppermute | solution.py:13
  1384.4 24.4 %collective-permute-start.2 = (f32[2,1,128,128]{3,2,0,1:T(8,128)S(1)}, f32[2,1,128,128]{3,2,0,1:T(8,128)S(1)}, u32[]{:S(2)}, u32[]{:S(2)}) collective-permute-start(f32[2,1,128,128]{3,2,0,1:T(8,128)S(1)} %get-tuple-element.838), channel_id=1, source_target_pairs={{0,8},{8,16},{16,24},{24,32},{32,40},{40,48},{48,56},{56,64},{64,7... | collective-permute-start | bytes 393224 | tf_op jit(solution)/shard_map/while/body/eval_jaxpr/ppermute | solution.py:13
  (98 other events, 1365.8 us)
where the time goes:
time: 1440 us
  waiting for transfers between devices  907 us (63%)
  starting transfers between devices  244 us (17%)
  blocking collectives  186 us (13%)
  matrix products  59.8 us (4%)
  local copies, waits for them, and re-layouts  15.2 us (1%)
    ppermute x126, waiting for transfers between devices, shifted(): lax.ppermute(array, axis, [(i, (i + by) % length) for i in range(length)])  907 us
    ppermute x126, starting transfers between devices, shifted(): lax.ppermute(array, axis, [(i, (i + by) % length) for i in range(length)])  244 us
    all_gather x1, blocking collectives, body(): every_pos = lax.all_gather(positions, 'ctx', axis=0, tiled=True)  186 us
  transfers between devices with their start and end apart: 126, of which 94 were waited for; matrix products, arithmetic and copies ran while one was open for 6% of the time, Pallas kernels for 0%

commit v1 on v0

v1 whole, which is shorter than its diff:
```python
import math

import jax
import jax.numpy as jnp
from jax import lax
from jax.experimental import pallas as pl
from jax.experimental.pallas import tpu as pltpu
from jax.sharding import PartitionSpec as P

SIDE = 4
SPAN = 64
DIM = 128
GROUP = 4
ROWS = SPAN * GROUP
KEYS = SPAN * SIDE
LOG2E = 1.4426950408889634
SCALE = 1.0 / math.sqrt(DIM)
F32 = jnp.float32
BF16 = jnp.bfloat16
MESH = pl.DeviceIdType.MESH


def dot_nt(a, b):
    return lax.dot_general(a, b, (((1,), (1,)), ((), ())), preferred_element_type=F32)


def dot_nn(a, b):
    return jnp.dot(a, b, preferred_element_type=F32)


class Links:
    def __init__(self, send_sems, recv_sems):
        self.send_sems = send_sems
        self.recv_sems = recv_sems
        self.count = 0
        self.made = []

    def copy(self, src, dst, device):
        made = pltpu.make_async_remote_copy(
            src_ref=src,
            dst_ref=dst,
            send_sem=self.send_sems.at[self.count],
            recv_sem=self.recv_sems.at[self.count],
            device_id={"ctx": device},
            device_id_type=MESH,
        )
        self.count += 1
        self.made.append(made)
        return made


def kernel(
    q_in, k_in, v_in, g_in, st_in, pos_in,
    dq_out, dk_out, dv_out,
    qd, kv, meta, stats, pos, kt, acc, dqt,
    part, relay, ybuf, zpart, zbuf, xpart, xrelay, xbuf,
    local_sems, send_sems, recv_sems,
):
    me = lax.axis_index("ctx")
    z, x, y = me // (SIDE * SIDE), (me // SIDE) % SIDE, me % SIDE

    def at(dz=0, dx=0, dy=0):
        return (
            ((z + dz) % SIDE) * (SIDE * SIDE) + ((x + dx) % SIDE) * SIDE + (y + dy) % SIDE
        )

    peers = [at(dx=1), at(dx=2), at(dx=3), at(dy=1), at(dy=3), at(dz=1), at(dz=2), at(dz=3)]

    loads = [
        pltpu.make_async_copy(q_in, qd.at[0, 0], local_sems.at[0]),
        pltpu.make_async_copy(g_in, qd.at[0, 1], local_sems.at[1]),
        pltpu.make_async_copy(k_in, kv.at[0, pl.ds(0, 128)], local_sems.at[2]),
        pltpu.make_async_copy(v_in, kv.at[0, pl.ds(128, 128)], local_sems.at[3]),
        pltpu.make_async_copy(st_in, stats, local_sems.at[4]),
        pltpu.make_async_copy(pos_in, pos, local_sems.at[5]),
    ]
    for load in loads:
        load.start()
    barrier = pltpu.get_barrier_semaphore()
    for peer in peers:
        pl.semaphore_signal(barrier, inc=1, device_id={"ctx": peer}, device_id_type=MESH)

    for load in loads:
        load.wait()
    span = (pos[0:1, 0:1] // SPAN).astype(F32)
    kv[0, 256:272, :] = jnp.broadcast_to(span, (16, DIM)).astype(BF16)
    spread_t = lax.broadcasted_iota(jnp.int32, (128, 512), 0)
    spread_r = lax.broadcasted_iota(jnp.int32, (128, 512), 1)
    spread = jnp.where(spread_r // GROUP == spread_t, 1.0, 0.0).astype(F32)
    wide = jnp.dot(
        stats[...], spread, preferred_element_type=F32, precision=lax.Precision.HIGHEST
    )
    head_of = lax.broadcasted_iota(jnp.int32, (8, 512), 0) % GROUP
    lane_of = lax.broadcasted_iota(jnp.int32, (8, 512), 1) % GROUP
    wide = jnp.where(head_of == lane_of, wide, 0.0)
    meta[0, 0:1, :] = jnp.sum(wide[0:4], axis=0, keepdims=True) * LOG2E
    meta[0, 1:2, :] = jnp.sum(wide[4:8], axis=0, keepdims=True)
    meta[0, 2:3, :] = jnp.broadcast_to(span, (1, 512))
    meta[0, 3:8, :] = jnp.zeros((5, 512), F32)

    pl.semaphore_wait(barrier, len(peers))

    links = Links(send_sems, recv_sems)
    q_right = links.copy(qd.at[0, 0], qd.at[3, 0], at(dx=1))
    g_left = links.copy(qd.at[0, 1], qd.at[1, 1], at(dx=3))
    g_right = links.copy(qd.at[0, 1], qd.at[3, 1], at(dx=1))
    q_left = links.copy(qd.at[0, 0], qd.at[1, 0], at(dx=3))
    q_on = links.copy(qd.at[3, 0], qd.at[2, 0], at(dx=1))
    g_on = links.copy(qd.at[1, 1], qd.at[2, 1], at(dx=3))
    meta_go = [links.copy(meta.at[0], meta.at[SIDE - s], at(dx=s)) for s in range(1, SIDE)]
    z_go = [
        links.copy(kv.at[0], kv.at[SIDE * (SIDE - s)], at(dz=s)) for s in range(1, SIDE)
    ]
    y_go = []
    for c in range(SIDE):
        k_part, v_part = pl.ds(0, 128), pl.ds(128, 144)
        b = SIDE * c
        y_go.append(
            dict(
                k_right=links.copy(kv.at[b, k_part], kv.at[b + 3, k_part], at(dy=1)),
                v_left=links.copy(kv.at[b, v_part], kv.at[b + 1, v_part], at(dy=3)),
                v_right=links.copy(kv.at[b, v_part], kv.at[b + 3, v_part], at(dy=1)),
                k_left=links.copy(kv.at[b, k_part], kv.at[b + 1, k_part], at(dy=3)),
                k_on=links.copy(kv.at[b + 3, k_part], kv.at[b + 2, k_part], at(dy=1)),
                v_on=links.copy(kv.at[b + 1, v_part], kv.at[b + 2, v_part], at(dy=3)),
            )
        )
    r_go = []
    k_rows, v_rows = pl.ds(0, 128), pl.ds(128, 128)
    for c in range(SIDE):
        r_go.append(
            dict(
                k_relay=links.copy(part.at[c, 1, k_rows], relay.at[c, 0], at(dy=1)),
                v_relay=links.copy(part.at[c, 1, v_rows], relay.at[c, 1], at(dy=3)),
                v_right=links.copy(part.at[c, 0, v_rows], ybuf.at[c, 0, v_rows], at(dy=1)),
                k_left=links.copy(part.at[c, 2, k_rows], ybuf.at[c, 1, k_rows], at(dy=3)),
                k_right=links.copy(part.at[c, 0, k_rows], ybuf.at[c, 0, k_rows], at(dy=1)),
                v_left=links.copy(part.at[c, 2, v_rows], ybuf.at[c, 1, v_rows], at(dy=3)),
            )
        )
    rz_go = [None] + [links.copy(zpart.at[s - 1], zbuf.at[s - 1], at(dz=s)) for s in range(1, SIDE)]
    dq_go = dict(
        e_relay=links.copy(xpart.at[1, k_rows], xrelay.at[0], at(dx=1)),
        l_relay=links.copy(xpart.at[1, v_rows], xrelay.at[1], at(dx=3)),
        l_right=links.copy(xpart.at[0, v_rows], xbuf.at[0, v_rows], at(dx=1)),
        e_left=links.copy(xpart.at[2, k_rows], xbuf.at[1, k_rows], at(dx=3)),
        e_right=links.copy(xpart.at[0, k_rows], xbuf.at[0, k_rows], at(dx=1)),
        l_left=links.copy(xpart.at[2, v_rows], xbuf.at[1, v_rows], at(dx=3)),
    )

    for s in range(SIDE - 1):
        z_go[s].start()
    for copy in (q_right, g_left):
        copy.start()
    for name in ("k_right", "v_left", "v_right", "k_left"):
        y_go[0][name].start()
    for copy in meta_go:
        copy.start()
    for copy in (g_right, q_left):
        copy.start()

    acc[...] = jnp.zeros_like(acc)
    dqt[...] = jnp.zeros_like(dqt)

    for c in range(1, SIDE):
        z_go[SIDE - 1 - c].wait_recv()
        for name in ("k_right", "v_left", "v_right", "k_left"):
            y_go[c][name].start()
    q_right.wait_recv()
    q_on.start()
    g_left.wait_recv()
    g_on.start()
    for c in range(SIDE):
        y_go[c]["k_right"].wait_recv()
        y_go[c]["k_on"].start()
        y_go[c]["v_left"].wait_recv()
        y_go[c]["v_on"].start()

    def probs_of(scores, log_total):
        return jnp.exp2(scores * (SCALE * LOG2E) - log_total)

    def own_early():
        key, value = kv[0, 0:64, :], kv[0, 128:192, :]
        query, grad = qd[0, 0, 0:ROWS, :], qd[0, 1, 0:ROWS, :]
        row_k = lax.broadcasted_iota(jnp.int32, (SPAN, ROWS), 0)
        col_r = lax.broadcasted_iota(jnp.int32, (SPAN, ROWS), 1) // GROUP
        scores = dot_nt(key, query) * (SCALE * LOG2E) - meta[0, 0:1, 0:ROWS]
        probs = jnp.exp2(jnp.where(row_k <= col_r, scores, -1e30))
        grad_probs = dot_nt(value, grad)
        grad_scores = (probs * (grad_probs - meta[0, 1:2, 0:ROWS])).astype(BF16)
        acc[0, 128:192, :] += dot_nn(probs.astype(BF16), grad)
        acc[0, 0:64, :] += dot_nn(grad_scores, query)
        dqt[0, 0:128, :] += dot_nn(key.T, grad_scores)

    def step(d, c, own):
        base = SIDE * c
        slots = pl.ds(base, SIDE)

        def rows(start):
            return kv[slots, start : start + SPAN, :].reshape(KEYS, DIM)

        k_e, k_l, v_e, v_l = rows(0), rows(64), rows(128), rows(192)
        q_e, q_l = qd[d, 0, 0:ROWS, :], qd[d, 0, ROWS : 2 * ROWS, :]
        g_e, g_l = qd[d, 1, 0:ROWS, :], qd[d, 1, ROWS : 2 * ROWS, :]
        lse_e, lse_l = meta[d, 0:1, 0:ROWS], meta[d, 0:1, ROWS : 2 * ROWS]
        del_e, del_l = meta[d, 1:2, 0:ROWS], meta[d, 1:2, ROWS : 2 * ROWS]
        span_k = kv[slots, 256:272, :].astype(F32)[:, 0:1, :]
        span_q = meta[d, 2:3, 0:DIM]
        low = jnp.where(span_k < span_q[None], 1.0, 0.0)
        low_rows = jnp.broadcast_to(low, (SIDE, SPAN, DIM)).reshape(KEYS, DIM)
        high_rows = 1.0 - low_rows
        low_wide = jnp.concatenate([low, low], axis=2)
        lane_block = lax.broadcasted_iota(jnp.int32, (1, KEYS), 1) // SPAN
        low_lane = jnp.zeros((1, KEYS), F32)
        for e in range(SIDE):
            low_lane = jnp.where(lane_block == e, low_wide[e], low_lane)

        @pl.when(d == 0)
        def _():
            kt[c, 0:128, :] = k_e.T
            kt[c, 128:256, :] = k_l.T

        probs = probs_of(dot_nt(k_e, q_l), lse_l)
        grad_probs = dot_nt(v_e, g_l)
        grad_scores = (probs * (grad_probs - del_l)).astype(BF16)
        dv_e = dot_nn(probs.astype(BF16), g_l)
        dk_e = dot_nn(grad_scores, q_l)
        dq_l = dot_nn(kt[c, 0:128, :], grad_scores)

        low_b, high_b = low_rows.astype(BF16), high_rows.astype(BF16)
        k_cat = jnp.concatenate([k_e * low_b, k_l * high_b], axis=1)
        v_cat = jnp.concatenate([v_e * low_b, v_l * high_b], axis=1)
        q_cat = jnp.concatenate([q_e, q_l], axis=1)
        g_cat = jnp.concatenate([g_e, g_l], axis=1)
        lse = jnp.where(low_wide > 0.5, lse_e[None], lse_l[None])
        delta = jnp.where(low_wide > 0.5, del_e[None], del_l[None])
        scores = dot_nt(k_cat, q_cat).reshape(SIDE, SPAN, ROWS) * (SCALE * LOG2E) - lse
        row_k = lax.broadcasted_iota(jnp.int32, (SPAN, ROWS), 0)
        col_r = lax.broadcasted_iota(jnp.int32, (SPAN, ROWS), 1) // GROUP
        seen = row_k <= col_r + jnp.where(own, 0, SPAN)
        first = jnp.where(seen, scores[0], -1e30)
        scores = jnp.concatenate([first[None], scores[1:]], axis=0)
        probs = jnp.exp2(scores)
        grad_probs = dot_nt(v_cat, g_cat).reshape(SIDE, SPAN, ROWS)
        grad_scores = (probs * (grad_probs - delta)).astype(BF16).reshape(KEYS, ROWS)
        probs = probs.astype(BF16).reshape(KEYS, ROWS)
        dv = dot_nn(probs, g_cat)
        dk = dot_nn(grad_scores, q_cat)
        low_lane_b, high_lane_b = low_lane.astype(BF16), (1.0 - low_lane).astype(BF16)
        kt_cat = jnp.concatenate(
            [kt[c, 0:128, :] * low_lane_b, kt[c, 128:256, :] * high_lane_b], axis=0
        )
        dq = dot_nn(kt_cat, grad_scores)

        def add(start, value):
            acc[slots, start : start + SPAN, :] += value.reshape(SIDE, SPAN, DIM)

        add(0, dk_e + dk[:, 0:128] * low_rows)
        add(64, dk[:, 128:256] * high_rows)
        add(128, dv_e + dv[:, 0:128] * low_rows)
        add(192, dv[:, 128:256] * high_rows)
        dqt[d, 0:128, :] += dq[0:128]
        dqt[d, 128:256, :] += dq[128:256] + dq_l

    def send_y(c):
        b = SIDE * c
        part[c, 1] = acc[b + 2].astype(BF16)
        r_go[c]["k_relay"].start()
        r_go[c]["v_relay"].start()
        part[c, 0, 128:256] = acc[b + 1, 128:256].astype(BF16)
        r_go[c]["v_right"].start()
        part[c, 2, 0:128] = acc[b + 3, 0:128].astype(BF16)
        r_go[c]["k_left"].start()

    def relay_y(c):
        b = SIDE * c
        r_go[c]["k_relay"].wait_recv()
        part[c, 0, 0:128] = (acc[b + 1, 0:128] + relay[c, 0].astype(F32)).astype(BF16)
        r_go[c]["k_right"].start()
        r_go[c]["v_relay"].wait_recv()
        part[c, 2, 128:256] = (acc[b + 3, 128:256] + relay[c, 1].astype(F32)).astype(BF16)
        r_go[c]["v_left"].start()

    def sum_y(c):
        for name in ("v_right", "k_left", "k_right", "v_left"):
            r_go[c][name].wait_recv()
        return acc[SIDE * c] + ybuf[c, 0].astype(F32) + ybuf[c, 1].astype(F32)

    def send_z(c):
        zpart[c - 1] = sum_y(c).astype(BF16)
        rz_go[c].start()

    def loop_step(i, carry):
        j = i - SIDE
        m = j % 3
        c = jnp.where(i < SIDE, i, (j // 3 + 1) % SIDE)
        d = jnp.where(i < SIDE, 0, 2 - m + 3 * (m // 2))

        def before(n):
            return pl.when(i == n)

        for n in range(SIDE):

            @before(n)
            def _(n=n):
                if n == 0:
                    y_go[n]["v_right"].wait_recv()
                    y_go[n]["k_left"].wait_recv()
                    y_go[n]["k_on"].wait_recv()
                    y_go[n]["v_on"].wait_recv()
                    own_early()
                else:
                    y_go[n]["v_right"].wait_recv()
                    y_go[n]["k_left"].wait_recv()
                    y_go[n]["k_on"].wait_recv()
                    y_go[n]["v_on"].wait_recv()

        @before(SIDE)
        def _():
            for copy in [g_right, q_left, q_on, g_on] + meta_go:
                copy.wait_recv()

        step(d, c, i == 0)

        @pl.when(i == 6)
        def _():
            send_y(1)

        @pl.when(i == 9)
        def _():
            relay_y(1)
            send_y(2)

        @pl.when(i == 12)
        def _():
            send_z(1)
            relay_y(2)
            send_y(3)

        @pl.when(i == 13)
        def _():
            xpart[1] = dqt[2].astype(BF16)
            dq_go["e_relay"].start()
            dq_go["l_relay"].start()

        @pl.when(i == 14)
        def _():
            xpart[0, 128:256] = dqt[1, 128:256].astype(BF16)
            dq_go["l_right"].start()

        return carry

    lax.fori_loop(0, SIDE * SIDE, loop_step, 0)

    send_y(0)
    xpart[2, 0:128] = dqt[3, 0:128].astype(BF16)
    dq_go["e_left"].start()
    dq_go["e_relay"].wait_recv()
    xpart[0, 0:128] = (dqt[1, 0:128] + xrelay[0].astype(F32)).astype(BF16)
    dq_go["e_right"].start()
    dq_go["l_relay"].wait_recv()
    xpart[2, 128:256] = (dqt[3, 128:256] + xrelay[1].astype(F32)).astype(BF16)
    dq_go["l_left"].start()
    send_z(2)
    relay_y(3)
    send_z(3)
    relay_y(0)
    for name in ("l_right", "e_left", "e_right", "l_left"):
        dq_go[name].wait_recv()
    total = (dqt[0] + xbuf[0].astype(F32) + xbuf[1].astype(F32)) * SCALE
    dq_out[0:ROWS, :] = total[0:128].T.astype(BF16)
    dq_out[ROWS : 2 * ROWS, :] = total[128:256].T.astype(BF16)
    own = sum_y(0)
    for s in range(1, SIDE):
        rz_go[s].wait_recv()
        own = own + zbuf[s - 1].astype(F32)
    dk_out[...] = (own[0:128] * SCALE).astype(BF16)
    dv_out[...] = own[128:256].astype(BF16)
    for copy in links.made:
        copy.wait_send()


COPIES = 6 + 3 + 3 + 24 + 24 + 3 + 6


def body(queries, keys, values, grad_out, saved_stats, positions):
    any_spec = pl.BlockSpec(memory_space=pl.ANY)
    vmem_spec = pl.BlockSpec(memory_space=pltpu.VMEM)
    dq, dk, dv = pl.pallas_call(
        kernel,
        out_shape=(
            jax.ShapeDtypeStruct((512, DIM), BF16),
            jax.ShapeDtypeStruct((128, DIM), BF16),
            jax.ShapeDtypeStruct((128, DIM), BF16),
        ),
        in_specs=[any_spec] * 6,
        out_specs=(vmem_spec,) * 3,
        scratch_shapes=[
            pltpu.VMEM((4, 2, 512, DIM), BF16),
            pltpu.VMEM((16, 272, DIM), BF16),
            pltpu.VMEM((4, 8, 512), F32),
            pltpu.VMEM((8, 128), F32),
            pltpu.VMEM((1, 128), jnp.int32),
            pltpu.VMEM((4, 256, KEYS), BF16),
            pltpu.VMEM((16, 256, DIM), F32),
            pltpu.VMEM((4, 256, ROWS), F32),
            pltpu.VMEM((4, 3, 256, DIM), BF16),
            pltpu.VMEM((4, 2, 128, DIM), BF16),
            pltpu.VMEM((4, 2, 256, DIM), BF16),
            pltpu.VMEM((3, 256, DIM), BF16),
            pltpu.VMEM((3, 256, DIM), BF16),
            pltpu.VMEM((3, 256, ROWS), BF16),
            pltpu.VMEM((2, 128, ROWS), BF16),
            pltpu.VMEM((2, 256, ROWS), BF16),
            pltpu.SemaphoreType.DMA((6,)),
            pltpu.SemaphoreType.DMA((COPIES,)),
            pltpu.SemaphoreType.DMA((COPIES,)),
        ],
        compiler_params=pltpu.CompilerParams(
            collective_id=0, has_side_effects=True, vmem_limit_bytes=48 * 1024 * 1024
        ),
    )(
        queries.reshape(512, DIM),
        keys.reshape(128, DIM),
        values.reshape(128, DIM),
        grad_out.reshape(512, DIM),
        saved_stats.reshape(8, 128),
        positions.reshape(1, 128),
    )
    return dq.reshape(128, GROUP, DIM), dk.reshape(128, 1, DIM), dv.reshape(128, 1, DIM)


def solution(mesh):
    in_specs = (
        P("ctx", "tp", None),
        P("ctx", "tp", None),
        P("ctx", "tp", None),
        P("ctx", "tp", None),
        P(None, "tp", "ctx"),
        P("ctx"),
    )
    out_specs = (P("ctx", "tp", None), P("ctx", "tp", None), P("ctx", "tp", None))
    return jax.shard_map(body, mesh=mesh, in_specs=in_specs, out_specs=out_specs, check_vma=False)
```

time: 1440 us -> 56.4 us (0.04)
  waiting for transfers between devices: 907 us -> 0 us
  starting transfers between devices: 244 us -> 0 us
  blocking collectives: 186 us -> 0 us
  matrix products: 59.8 us -> 0 us
  Pallas kernels: 0 us -> 49.5 us
    ppermute x126 -> x0, waiting for transfers between devices: 907 us -> none  [shifted(): lax.ppermute(array, axis, [(i, (i + by) % length) for i in range(length)])]
    ppermute x126 -> x0, starting transfers between devices: 244 us -> none  [shifted(): lax.ppermute(array, axis, [(i, (i + by) % length) for i in range(length)])]
    all_gather x1 -> x0, blocking collectives: 186 us -> none  [body(): every_pos = lax.all_gather(positions, 'ctx', axis=0, tiled=True)]
    dot_general x325 -> x0, matrix products: 59.8 us -> none  [the longest x65 15.3 us: backward_tile(): jnp.einsum('bhkr,bhkd->bhrd', grad_scores, key_rows, preferred_element_ty...]
    pallas_call x0 -> x1, Pallas kernels: none -> 49.5 us  [body(): pl.pallas_call(kernel, out_shape=(jax.ShapeDtypeStruct((512, DIM), BF16),...]
  transfers between devices with their start and end apart: 126 -> 0, of which waited for: 94 -> 0; matrix products, arithmetic and copies ran while one was open for 6% -> 0% of each run, Pallas kernels for 0% -> 0%
where the time goes in v1:
time: 56.4 us; the launch traced here: 56.1 us
  Pallas kernels  49.5 us (88%)
  local copies, waits for them, and re-layouts  5.88 us (10%)
  between operations  0.66 us (1%)
    pallas_call x1, Pallas kernels, body(): pl.pallas_call(kernel, out_shape=(jax.ShapeDtypeStruct((512, DIM), BF16),...  49.5 us
    unnamed x15, local copies, waits for them, and re-layouts  5.88 us

profile of v1, /device:TPU:128, one launch (start us, length us, event | category | flops | bytes accessed | tf_op | source)
XLA Modules:
  0.0 56.1 jit_solution(13375006544125102104)
XLA Ops:
  0.6 0.0 copy-start.4
  0.6 0.0 copy-start.5
  0.7 0.7 %copy-done.4 = f32[2,4,128]{2,1,0:T(4,128)S(1)} copy-done((f32[2,4,128]{2,1,0:T(4,128)S(1)}, f32[2,4,128]{2,1,0:T(4,128)}, u32[]{:S(2)}) %copy-start.4) | copy-done | bytes 4120
  1.3 0.0 copy-done.5
  1.3 0.0 copy-start
  1.3 0.9 %copy-done = bf16[128,4,128]{2,1,0:T(4,128)(2,1)S(1)} copy-done((bf16[128,4,128]{2,1,0:T(4,128)(2,1)S(1)}, bf16[128,4,128]{2,1,0:T(4,128)(2,1)}, u32[]{:S(2)}) %copy-start) | copy-done | bytes 131096
  2.2 0.0 copy-start.1
  2.2 0.9 %copy-done.1 = bf16[128,4,128]{2,1,0:T(4,128)(2,1)S(1)} copy-done((bf16[128,4,128]{2,1,0:T(4,128)(2,1)S(1)}, bf16[128,4,128]{2,1,0:T(4,128)(2,1)}, u32[]{:S(2)}) %copy-start.1) | copy-done | bytes 131096
  3.1 0.0 copy-start.2
  3.1 0.8 %copy-done.2 = bf16[128,1,128]{2,0,1:T(8,128)(2,1)S(1)} copy-done((bf16[128,1,128]{2,0,1:T(8,128)(2,1)S(1)}, bf16[128,1,128]{2,0,1:T(8,128)(2,1)}, u32[]{:S(2)}) %copy-start.2) | copy-done | bytes 32792
  3.9 0.0 copy-start.3
  3.9 0.8 %copy-done.3 = bf16[128,1,128]{2,0,1:T(8,128)(2,1)S(1)} copy-done((bf16[128,1,128]{2,0,1:T(8,128)(2,1)S(1)}, bf16[128,1,128]{2,0,1:T(8,128)(2,1)}, u32[]{:S(2)}) %copy-start.3) | copy-done | bytes 32792
  4.6 49.5 %shard_map.85 = (bf16[512,128]{1,0:T(8,128)(2,1)S(1)}, bf16[128,128]{1,0:T(8,128)(2,1)S(1)}, bf16[128,128]{1,0:T(8,128)(2,1)S(1)}) custom-call(bf16[512,128]{1,0:T(8,128)(2,1)S(1)} %bitcast.9, bf16[128,128]{1,0:T(8,128)(2,1)S(1)} %bitcast.14, bf16[128,128]{1,0:T(8,128)(2,1)S(1)} %bitcast.15, bf16[512,128]{1,0:T(8,128)(2,1)S(1)} %bitcast.10, ...), custom_call_target="tpu_custom_call" | custom-call | tf_op jit(solution)/shard_map/pallas_call | solution.py:389
  54.2 0.7 %copy.12 = bf16[128,4,128]{2,1,0:T(4,128)(2,1)} copy(bf16[128,4,128]{2,1,0:T(4,128)(2,1)S(1)} %bitcast.11) | data formatting | bytes 262144
  54.8 0.6 %copy.13 = bf16[128,1,128]{2,0,1:T(8,128)(2,1)} copy(bf16[128,1,128]{2,0,1:T(8,128)(2,1)S(1)} %bitcast.13) | data formatting | bytes 65536
  55.4 0.6 %copy.14 = bf16[128,1,128]{2,0,1:T(8,128)(2,1)} copy(bf16[128,1,128]{2,0,1:T(8,128)(2,1)S(1)} %bitcast.12) | data formatting | bytes 65536
Async XLA Ops:
  0.6 0.7 %copy-start.4 = (f32[2,4,128]{2,1,0:T(4,128)S(1)}, f32[2,4,128]{2,1,0:T(4,128)}, u32[]{:S(2)}) copy-start(f32[2,4,128]{2,1,0:T(4,128)} %param.10) | copy-start | bytes 12292
  0.6 0.7 %copy-start.5 = (s32[128]{0:T(128)S(1)}, s32[128]{0:T(128)}, u32[]{:S(2)}) copy-start(s32[128]{0:T(128)} %param.11) | copy-start | bytes 1540
  1.3 0.9 %copy-start = (bf16[128,4,128]{2,1,0:T(4,128)(2,1)S(1)}, bf16[128,4,128]{2,1,0:T(4,128)(2,1)}, u32[]{:S(2)}) copy-start(bf16[128,4,128]{2,1,0:T(4,128)(2,1)} %param.6) | copy-start | bytes 393220
  2.2 0.9 %copy-start.1 = (bf16[128,4,128]{2,1,0:T(4,128)(2,1)S(1)}, bf16[128,4,128]{2,1,0:T(4,128)(2,1)}, u32[]{:S(2)}) copy-start(bf16[128,4,128]{2,1,0:T(4,128)(2,1)} %param.9) | copy-start | bytes 393220
  3.1 0.8 %copy-start.2 = (bf16[128,1,128]{2,0,1:T(8,128)(2,1)S(1)}, bf16[128,1,128]{2,0,1:T(8,128)(2,1)}, u32[]{:S(2)}) copy-start(bf16[128,1,128]{2,0,1:T(8,128)(2,1)} %param.7) | copy-start | bytes 98308
  3.9 0.8 %copy-start.3 = (bf16[128,1,128]{2,0,1:T(8,128)(2,1)S(1)}, bf16[128,1,128]{2,0,1:T(8,128)(2,1)}, u32[]{:S(2)}) copy-start(bf16[128,1,128]{2,0,1:T(8,128)(2,1)} %param.8) | copy-start | bytes 98308

commit v2 on v1

v2 whole, which is shorter than its diff:
```python
import math

import jax
import jax.numpy as jnp
from jax import lax
from jax.experimental import pallas as pl
from jax.experimental.pallas import tpu as pltpu
from jax.sharding import PartitionSpec as P

SIDE = 4
SPAN = 64
DIM = 128
GROUP = 4
ROWS = SPAN * GROUP
KEYS = SPAN * SIDE
LOG2E = 1.4426950408889634
SCALE = 1.0 / math.sqrt(DIM)
F32 = jnp.float32
BF16 = jnp.bfloat16
MESH = pl.DeviceIdType.MESH


def dot_nt(a, b):
    return lax.dot_general(a, b, (((1,), (1,)), ((), ())), preferred_element_type=F32)


def dot_tn(a, b):
    return lax.dot_general(a, b, (((0,), (0,)), ((), ())), preferred_element_type=F32)


def dot_nn(a, b):
    return jnp.dot(a, b, preferred_element_type=F32)


class Links:
    def __init__(self, send_sems, recv_sems):
        self.send_sems = send_sems
        self.recv_sems = recv_sems
        self.count = 0
        self.made = []

    def copy(self, src, dst, device):
        made = pltpu.make_async_remote_copy(
            src_ref=src,
            dst_ref=dst,
            send_sem=self.send_sems.at[self.count],
            recv_sem=self.recv_sems.at[self.count],
            device_id={"ctx": device},
            device_id_type=MESH,
        )
        self.count += 1
        self.made.append(made)
        return made


def kernel(
    q_in, k_in, v_in, g_in, st_in, pos_in,
    out,
    qd, kv, meta, stats, pos, qt, acc, dqt,
    part, ybuf, zpart, zbuf, xpart, xbuf,
    local_sems, send_sems, recv_sems,
):
    me = lax.axis_index("ctx")
    z, x, y = me // (SIDE * SIDE), (me // SIDE) % SIDE, me % SIDE

    def at(dz=0, dx=0, dy=0):
        return (
            ((z + dz) % SIDE) * (SIDE * SIDE) + ((x + dx) % SIDE) * SIDE + (y + dy) % SIDE
        )

    peers = [at(dx=1), at(dx=2), at(dx=3), at(dy=1), at(dy=2), at(dy=3), at(dz=1), at(dz=2), at(dz=3)]

    loads = [
        pltpu.make_async_copy(q_in, qd.at[0, 0], local_sems.at[0]),
        pltpu.make_async_copy(g_in, qd.at[0, 1], local_sems.at[1]),
        pltpu.make_async_copy(k_in, kv.at[0, pl.ds(0, 128)], local_sems.at[2]),
        pltpu.make_async_copy(v_in.at[pl.ds(0, 64)], kv.at[0, pl.ds(128, 64)], local_sems.at[3]),
        pltpu.make_async_copy(v_in.at[pl.ds(64, 64)], kv.at[0, pl.ds(208, 64)], local_sems.at[6]),
        pltpu.make_async_copy(st_in, stats, local_sems.at[4]),
        pltpu.make_async_copy(pos_in, pos, local_sems.at[5]),
    ]
    for load in loads:
        load.start()
    barrier = pltpu.get_barrier_semaphore()
    for peer in peers:
        pl.semaphore_signal(barrier, inc=1, device_id={"ctx": peer}, device_id_type=MESH)

    for load in loads[2:5] + loads[6:]:
        load.wait()
    span = (pos[0:1, 0:1] // SPAN).astype(F32)
    kv[0, 192:208, :] = jnp.broadcast_to(span, (16, DIM)).astype(BF16)

    links = Links(send_sems, recv_sems)
    q_go = [None] + [
        [links.copy(qd.at[0, n], qd.at[s, n], at(dx=SIDE - s)) for n in range(2)]
        for s in range(1, SIDE)
    ]
    meta_go = [None] + [
        links.copy(meta.at[0], meta.at[s], at(dx=SIDE - s)) for s in range(1, SIDE)
    ]
    z_go = [None] + [
        links.copy(kv.at[0], kv.at[SIDE * s], at(dz=SIDE - s)) for s in range(1, SIDE)
    ]
    y_go = [
        [links.copy(kv.at[SIDE * c], kv.at[SIDE * c + s], at(dy=SIDE - s)) for s in range(1, SIDE)]
        for c in range(SIDE)
    ]
    ry_go = [
        [links.copy(part.at[c, s - 1], ybuf.at[c, s - 1], at(dy=s)) for s in range(1, SIDE)]
        for c in range(SIDE)
    ]
    rz_go = [None] + [
        links.copy(zpart.at[s - 1], zbuf.at[s - 1], at(dz=s)) for s in range(1, SIDE)
    ]
    rx_go = [None] + [
        links.copy(xpart.at[s - 1], xbuf.at[s - 1], at(dx=s)) for s in range(1, SIDE)
    ]

    def start(copies):
        for copy in copies:
            copy.start()

    def arrive(copies):
        for copy in copies:
            copy.wait_recv()

    pl.semaphore_wait(barrier, len(peers))
    start((z_go[1], z_go[3], z_go[2]))
    start(y_go[0])
    for load in loads[0:2]:
        load.wait()
    start(q_go[1])
    start(q_go[3])

    loads[5].wait()
    spread_t = lax.broadcasted_iota(jnp.int32, (128, 512), 0)
    spread_r = lax.broadcasted_iota(jnp.int32, (128, 512), 1)
    spread = jnp.where(spread_r // GROUP == spread_t, 1.0, 0.0).astype(F32)
    wide = jnp.dot(
        stats[...], spread, preferred_element_type=F32, precision=lax.Precision.HIGHEST
    )
    head_of = lax.broadcasted_iota(jnp.int32, (8, 512), 0) % GROUP
    lane_of = lax.broadcasted_iota(jnp.int32, (8, 512), 1) % GROUP
    wide = jnp.where(head_of == lane_of, wide, 0.0)
    meta[0, 0:1, :] = jnp.sum(wide[0:4], axis=0, keepdims=True) * LOG2E
    meta[0, 1:2, :] = jnp.sum(wide[4:8], axis=0, keepdims=True)
    meta[0, 2:3, :] = jnp.broadcast_to(span, (1, 512))
    meta[0, 3:8, :] = jnp.zeros((5, 512), F32)
    start(meta_go[1:])

    for c in (1, 3, 2):
        arrive([z_go[c]])
        start(y_go[c])
    start(q_go[2])

    acc[...] = jnp.zeros_like(acc)
    dqt[...] = jnp.zeros_like(dqt)

    def probs_of(scores, log_total):
        return jnp.exp2(scores * (SCALE * LOG2E) - log_total)

    def turn(d):
        for n in range(2):
            qt[d, n, 0:128, :] = qd[d, n, 0:ROWS, :].T
            qt[d, n, 128:256, :] = qd[d, n, ROWS : 2 * ROWS, :].T

    def own_early():
        key, value = kv[0, 0:64, :], kv[0, 128:192, :]
        query, grad = qd[0, 0, 0:ROWS, :], qd[0, 1, 0:ROWS, :]
        row_k = lax.broadcasted_iota(jnp.int32, (SPAN, ROWS), 0)
        col_r = lax.broadcasted_iota(jnp.int32, (SPAN, ROWS), 1) // GROUP
        scores = dot_nt(key, query) * (SCALE * LOG2E) - meta[0, 0:1, 0:ROWS]
        probs = jnp.exp2(jnp.where(row_k <= col_r, scores, -1e30))
        grad_probs = dot_nt(value, grad)
        grad_scores = (probs * (grad_probs - meta[0, 1:2, 0:ROWS])).astype(BF16)
        acc[0, 128:192, :] += dot_nn(probs.astype(BF16), grad)
        acc[0, 0:64, :] += dot_nn(grad_scores, query)
        dqt[0, 0:128, :] += dot_tn(key, grad_scores)

    def step(group, c, own):
        base = SIDE * c
        slots = pl.ds(base, SIDE)

        def rows(start):
            return kv[slots, start : start + SPAN, :].reshape(KEYS, DIM)

        k_e, k_l, v_e, v_l = rows(0), rows(64), rows(128), rows(208)
        span_k = kv[slots, 192:208, :].astype(F32)[:, 0:1, :]
        st = []
        for d in group:
            q_e, q_l = qd[d, 0, 0:ROWS, :], qd[d, 0, ROWS : 2 * ROWS, :]
            g_e, g_l = qd[d, 1, 0:ROWS, :], qd[d, 1, ROWS : 2 * ROWS, :]
            span_q = meta[d, 2:3, 0:DIM]
            low = jnp.where(span_k < span_q[None], 1.0, 0.0)
            low_rows = jnp.broadcast_to(low, (SIDE, SPAN, DIM)).reshape(KEYS, DIM)
            high_rows = 1.0 - low_rows
            low_wide = jnp.concatenate([low, low], axis=2)
            low_b, high_b = low_rows.astype(BF16), high_rows.astype(BF16)
            k_cat = jnp.concatenate([k_e * low_b, k_l * high_b], axis=1)
            v_cat = jnp.concatenate([v_e * low_b, v_l * high_b], axis=1)
            s1 = dot_nn(k_e, qt[d, 0, 128:256, :])
            p1 = dot_nn(v_e, qt[d, 1, 128:256, :])
            s2 = dot_nn(k_cat, qt[d, 0])
            p2 = dot_nn(v_cat, qt[d, 1])
            st.append((d, low_rows, high_rows, low_wide, k_cat, s1, p1, s2, p2, q_e, q_l, g_e, g_l))
        tot = None
        for (d, low_rows, high_rows, low_wide, k_cat, s1, p1, s2, p2, q_e, q_l, g_e, g_l) in st:
            lse_e, lse_l = meta[d, 0:1, 0:ROWS], meta[d, 0:1, ROWS : 2 * ROWS]
            del_e, del_l = meta[d, 1:2, 0:ROWS], meta[d, 1:2, ROWS : 2 * ROWS]
            probs = probs_of(s1, lse_l)
            grad_scores = (probs * (p1 - del_l)).astype(BF16)
            dv_e = dot_nn(probs.astype(BF16), g_l)
            dk_e = dot_nn(grad_scores, q_l)
            dq_l = dot_tn(k_e, grad_scores)
            q_cat = jnp.concatenate([q_e, q_l], axis=1)
            g_cat = jnp.concatenate([g_e, g_l], axis=1)
            lse = jnp.where(low_wide > 0.5, lse_e[None], lse_l[None])
            delta = jnp.where(low_wide > 0.5, del_e[None], del_l[None])
            scores = s2.reshape(SIDE, SPAN, ROWS) * (SCALE * LOG2E) - lse
            row_k = lax.broadcasted_iota(jnp.int32, (SPAN, ROWS), 0)
            col_r = lax.broadcasted_iota(jnp.int32, (SPAN, ROWS), 1) // GROUP
            seen = row_k <= col_r + jnp.where(own, 0, SPAN)
            first = jnp.where(seen, scores[0], -1e30)
            scores = jnp.concatenate([first[None], scores[1:]], axis=0)
            probs = jnp.exp2(scores)
            grad_probs = p2.reshape(SIDE, SPAN, ROWS)
            grad_scores = (probs * (grad_probs - delta)).astype(BF16).reshape(KEYS, ROWS)
            probs = probs.astype(BF16).reshape(KEYS, ROWS)
            dv = dot_nn(probs, g_cat)
            dk = dot_nn(grad_scores, q_cat)
            dq = dot_tn(k_cat, grad_scores)
            dqt[d, 0:128, :] += dq[0:128]
            dqt[d, 128:256, :] += dq[128:256] + dq_l
            parts = [dk_e + dk[:, 0:128] * low_rows, dk[:, 128:256] * high_rows, dv_e + dv[:, 0:128] * low_rows, dv[:, 128:256] * high_rows]
            tot = parts if tot is None else [x + y for x, y in zip(tot, parts)]
            own = False
        for n in range(4):
            acc[slots, SPAN * n : SPAN * (n + 1), :] += tot[n].reshape(SIDE, SPAN, DIM)

    def send_y(c):
        for n in range(1, SIDE):
            part[c, n - 1] = acc[SIDE * c + n].astype(BF16)
            ry_go[c][n - 1].start()

    def sum_y(c):
        arrive(ry_go[c])
        total = acc[SIDE * c]
        for n in range(SIDE - 1):
            total = total + ybuf[c, n].astype(F32)
        return total

    def send_z(c):
        zpart[c - 1] = sum_y(c).astype(BF16)
        rz_go[c].start()

    def send_x(d):
        xpart[d - 1] = dqt[d].astype(BF16)
        rx_go[d].start()

    def pick(i, table):
        value = jnp.int32(table[-1])
        for n, entry in enumerate(table[:-1]):
            value = jnp.where(i == n, entry, value)
        return value

    def finish_x():
        arrive(rx_go[1:])
        total = dqt[0]
        for n in range(SIDE - 1):
            total = total + xbuf[n].astype(F32)
        total = total * SCALE
        out[0:ROWS, :] = total[0:128].T.astype(BF16)
        out[ROWS : 2 * ROWS, :] = total[128:256].T.astype(BF16)

    def finish_kv():
        own = sum_y(0)
        arrive(rz_go[1:])
        for n in range(SIDE - 1):
            own = own + zbuf[n].astype(F32)
        out[512:640, :] = (own[0:128] * SCALE).astype(BF16)
        out[640:768, :] = own[128:256].astype(BF16)

    def need_q(d):
        arrive(q_go[d] + [meta_go[d]])
        turn(d)

    actions = {
        "need_y": lambda c: arrive(y_go[c]),
        "need_q": need_q,
        "send_y": send_y,
        "send_z": send_z,
        "send_x": send_x,
    }

    def act(names):
        for name in names:
            actions[name[:-1]](int(name[-1]))

    def loop_step(i, carry):
        for n in BEFORE:
            pl.when(i == n)(lambda n=n: act(BEFORE[n]))
        c = pick(i, [entry[1] for entry in ORDER])
        for group in GROUPS:
            chosen = pick(i, [int(entry[0] == group) for entry in ORDER])
            pl.when(chosen == 1)(lambda group=group: step(GROUPS[group], c, i == 0))
        for n in AFTER:
            pl.when(i == n)(lambda n=n: act(AFTER[n]))
        return carry

    turn(0)
    arrive(y_go[0])
    own_early()
    lax.fori_loop(0, len(ORDER), loop_step, 0)
    act(LAST)
    finish_x()
    finish_kv()
    for copy in links.made:
        copy.wait_send()


COPIES = 9 + 3 + 12 + 12 + 3 + 3
GROUPS = {"t": (0, 1, 3), "s": (2,)}
ORDER = (("t", 0), ("t", 1), ("t", 3), ("s", 1), ("s", 3), ("t", 2), ("s", 2), ("s", 0))
BEFORE = {0: ("need_q1", "need_q3"), 1: ("need_y1",), 2: ("need_y3",), 3: ("need_q2",), 5: ("need_y2",)}
AFTER = {3: ("send_y1",), 4: ("send_y3",), 5: ("send_x1", "send_x3"), 6: ("send_y2", "send_z1")}
LAST = ("send_x2", "send_y0", "send_z3", "send_z2")


def body(queries, keys, values, grad_out, saved_stats, positions):
    hbm_spec = pl.BlockSpec(memory_space=pltpu.HBM)
    vmem_spec = pl.BlockSpec(memory_space=pltpu.VMEM)
    grads = pl.pallas_call(
        kernel,
        out_shape=jax.ShapeDtypeStruct((768, DIM), BF16),
        in_specs=[hbm_spec] * 6,
        out_specs=vmem_spec,
        scratch_shapes=[
            pltpu.VMEM((4, 2, 512, DIM), BF16),
            pltpu.VMEM((16, 272, DIM), BF16),
            pltpu.VMEM((4, 8, 512), F32),
            pltpu.VMEM((8, 128), F32),
            pltpu.VMEM((1, 128), jnp.int32),
            pltpu.VMEM((4, 2, 256, ROWS), BF16),
            pltpu.VMEM((16, 256, DIM), F32),
            pltpu.VMEM((4, 256, ROWS), F32),
            pltpu.VMEM((4, 3, 256, DIM), BF16),
            pltpu.VMEM((4, 3, 256, DIM), BF16),
            pltpu.VMEM((3, 256, DIM), BF16),
            pltpu.VMEM((3, 256, DIM), BF16),
            pltpu.VMEM((3, 256, ROWS), BF16),
            pltpu.VMEM((3, 256, ROWS), BF16),
            pltpu.SemaphoreType.DMA((7,)),
            pltpu.SemaphoreType.DMA((COPIES,)),
            pltpu.SemaphoreType.DMA((COPIES,)),
        ],
        compiler_params=pltpu.CompilerParams(
            collective_id=0, has_side_effects=True, vmem_limit_bytes=62 * 1024 * 1024
        ),
    )(
        queries.reshape(512, DIM),
        keys.reshape(128, DIM),
        values.reshape(128, DIM),
        grad_out.reshape(512, DIM),
        saved_stats.reshape(8, 128),
        positions.reshape(1, 128),
    )
    return (
        grads[0:512].reshape(128, GROUP, DIM),
        grads[512:640].reshape(128, 1, DIM),
        grads[640:768].reshape(128, 1, DIM),
    )


def solution(mesh):
    in_specs = (
        P("ctx", "tp", None),
        P("ctx", "tp", None),
        P("ctx", "tp", None),
        P("ctx", "tp", None),
        P(None, "tp", "ctx"),
        P("ctx"),
    )
    out_specs = (P("ctx", "tp", None), P("ctx", "tp", None), P("ctx", "tp", None))
    return jax.shard_map(body, mesh=mesh, in_specs=in_specs, out_specs=out_specs, check_vma=False)
```

time: 56.4 us -> 42.5 us (0.75)
  Pallas kernels: 49.5 us -> 38.7 us
  local copies, waits for them, and re-layouts: 5.88 us -> 2.97 us
    pallas_call x1, Pallas kernels: 49.5 us -> 38.7 us  [body(): pl.pallas_call(kernel, out_shape=jax.ShapeDtypeStruct((768, DIM), BF16),...]
    unnamed x15 -> x0, local copies, waits for them, and re-layouts: 5.88 us -> none
    slice x0 -> x1, local copies, waits for them, and re-layouts: none -> 1.57 us  [body(): grads[0:512].reshape(128, GROUP, DIM)]
    reshape x0 -> x1, local copies, waits for them, and re-layouts: none -> 1.4 us  [body(): grads[640:768].reshape(128, 1, DIM)]
where the time goes in v2:
time: 42.5 us; the launch traced here: 42.3 us
  Pallas kernels  38.7 us (91%)
  local copies, waits for them, and re-layouts  2.97 us (7%)
  between operations  0.64 us (2%)
    pallas_call x1, Pallas kernels, body(): pl.pallas_call(kernel, out_shape=jax.ShapeDtypeStruct((768, DIM), BF16),...  38.7 us
    slice x1, local copies, waits for them, and re-layouts, body(): grads[0:512].reshape(128, GROUP, DIM)  1.57 us
    reshape x1, local copies, waits for them, and re-layouts, body(): grads[640:768].reshape(128, 1, DIM)  1.4 us

profile of v2, /device:TPU:128, one launch (start us, length us, event | category | flops | bytes accessed | tf_op | source)
XLA Modules:
  0.0 42.3 jit_solution(16229726509329152461)
XLA Ops:
  0.6 38.7 %shard_map.85 = bf16[768,128]{1,0:T(8,128)(2,1)} custom-call(bf16[512,128]{1,0:T(8,128)(2,1)} %bitcast.11, bf16[128,128]{1,0:T(8,128)(2,1)} %bitcast.14, bf16[128,128]{1,0:T(8,128)(2,1)} %bitcast.15, bf16[512,128]{1,0:T(8,128)(2,1)} %bitcast.12, f32[8,128]{1,0:T(8,128)} %bitcast.16, s32[1,128]{1,0:T(1,128)} %bitcast.17), custom_call_target="tpu_custom_call" | custom-call | tf_op jit(solution)/shard_map/pallas_call | solution.py:332
  39.3 1.4 %slice_bitcast_fusion = (bf16[128,1,128]{2,0,1:T(8,128)(2,1)}, bf16[128,1,128]{2,0,1:T(8,128)(2,1)}) fusion(bf16[768,128]{1,0:T(8,128)(2,1)} %shard_map.85), kind=kLoop, calls=%fused_computation | loop fusion | bytes 131072 | tf_op jit(solution)/shard_map/reshape | solution.py:370
  40.7 1.6 %slice.9 = bf16[512,128]{1,0:T(8,128)(2,1)} slice(bf16[768,128]{1,0:T(8,128)(2,1)} %shard_map.85), slice={[0:512], [0:128]} | slice | bytes 262144 | tf_op jit(solution)/shard_map/slice | solution.py:368

commit v3 on v2

--- a/solution.py
+++ b/solution.py
@@ -57,7 +57,7 @@
     q_in, k_in, v_in, g_in, st_in, pos_in,
     out,
     qd, kv, meta, stats, pos, qt, acc, dqt,
-    part, ybuf, zpart, zbuf, xpart, xbuf,
+    part, ybuf, zpart, zbuf, lpart, lbuf, xpart, xbuf,
     local_sems, send_sems, recv_sems,
 ):
     me = lax.axis_index("ctx")
@@ -91,26 +91,60 @@
     kv[0, 192:208, :] = jnp.broadcast_to(span, (16, DIM)).astype(BF16)
 
     links = Links(send_sems, recv_sems)
-    q_go = [None] + [
-        [links.copy(qd.at[0, n], qd.at[s, n], at(dx=SIDE - s)) for n in range(2)]
-        for s in range(1, SIDE)
-    ]
+    head, tail = pl.ds(0, 208), pl.ds(208, 64)
+    z_head = [None] + [
+        links.copy(kv.at[0, head], kv.at[SIDE * s, head], at(dz=SIDE - s)) for s in range(1, SIDE)
+    ]
+    z_tail = [None] + [
+        [
+            links.copy(kv.at[n, tail], kv.at[SIDE * s + n, tail], at(dz=SIDE - s))
+            for s in range(1, SIDE)
+        ]
+        for n in range(1, SIDE)
+    ]
+    z_tail[0] = [
+        links.copy(kv.at[0, tail], kv.at[SIDE * s, tail], at(dz=SIDE - s)) for s in range(1, SIDE)
+    ]
+    y_tail = [None] + [
+        links.copy(kv.at[0, tail], kv.at[s, tail], at(dy=SIDE - s)) for s in range(1, SIDE)
+    ]
+    y_head = [
+        [
+            links.copy(kv.at[SIDE * c, head], kv.at[SIDE * c + s, head], at(dy=SIDE - s))
+            for s in range(1, SIDE)
+        ]
+        for c in range(SIDE)
+    ]
+    halves = (pl.ds(0, ROWS), pl.ds(ROWS, ROWS))
+    q_right = [
+        [links.copy(qd.at[0, n, h], qd.at[3, n, h], at(dx=1)) for h in halves] for n in range(2)
+    ]
+    q_left = [
+        [links.copy(qd.at[0, n, h], qd.at[1, n, h], at(dx=3)) for h in halves] for n in range(2)
+    ]
+    on_right = [links.copy(qd.at[3, 0, h], qd.at[2, 0, h], at(dx=1)) for h in halves]
+    on_left = [links.copy(qd.at[1, 1, h], qd.at[2, 1, h], at(dx=3)) for h in halves]
     meta_go = [None] + [
         links.copy(meta.at[0], meta.at[s], at(dx=SIDE - s)) for s in range(1, SIDE)
     ]
-    z_go = [None] + [
-        links.copy(kv.at[0], kv.at[SIDE * s], at(dz=SIDE - s)) for s in range(1, SIDE)
-    ]
-    y_go = [
-        [links.copy(kv.at[SIDE * c], kv.at[SIDE * c + s], at(dy=SIDE - s)) for s in range(1, SIDE)]
+    q_come = [None, q_left[0], on_right + on_left, q_right[1]]
+    most, last = pl.ds(0, 192), pl.ds(192, 64)
+    ry_most = [
+        [
+            links.copy(part.at[c, s - 1, most], ybuf.at[c, s - 1, most], at(dy=s))
+            for s in range(1, SIDE)
+        ]
         for c in range(SIDE)
     ]
-    ry_go = [
-        [links.copy(part.at[c, s - 1], ybuf.at[c, s - 1], at(dy=s)) for s in range(1, SIDE)]
-        for c in range(SIDE)
-    ]
-    rz_go = [None] + [
+    ry_last = [
+        links.copy(part.at[0, s - 1, last], ybuf.at[0, s - 1, last], at(dy=s))
+        for s in range(1, SIDE)
+    ]
+    rz_most = [None] + [
         links.copy(zpart.at[s - 1], zbuf.at[s - 1], at(dz=s)) for s in range(1, SIDE)
+    ]
+    rz_last = [None] + [
+        links.copy(lpart.at[s - 1], lbuf.at[s - 1], at(dz=s)) for s in range(1, SIDE)
     ]
     rx_go = [None] + [
         links.copy(xpart.at[s - 1], xbuf.at[s - 1], at(dx=s)) for s in range(1, SIDE)
@@ -125,12 +159,16 @@
             copy.wait_recv()
 
     pl.semaphore_wait(barrier, len(peers))
-    start((z_go[1], z_go[3], z_go[2]))
-    start(y_go[0])
+    start((z_head[1], z_head[3], z_head[2]))
+    start(y_tail[1:])
+    start(y_head[0])
+    start(z_tail[0])
     for load in loads[0:2]:
         load.wait()
-    start(q_go[1])
-    start(q_go[3])
+    for h in range(2):
+        start((q_right[0][h], q_left[1][h]))
+    for h in range(2):
+        start((q_right[1][h], q_left[0][h]))
 
     loads[5].wait()
     spread_t = lax.broadcasted_iota(jnp.int32, (128, 512), 0)
@@ -148,10 +186,28 @@
     meta[0, 3:8, :] = jnp.zeros((5, 512), F32)
     start(meta_go[1:])
 
-    for c in (1, 3, 2):
-        arrive([z_go[c]])
-        start(y_go[c])
-    start(q_go[2])
+    def forward_q(h):
+        arrive([q_right[0][h]])
+        start([on_right[h]])
+        arrive([q_left[1][h]])
+        start([on_left[h]])
+
+    def forward_z(c):
+        arrive([z_head[c]])
+        start(y_head[c])
+
+    def forward_y(n):
+        arrive([y_tail[n]])
+        start(z_tail[n])
+
+    forward_z(1)
+    forward_q(0)
+    forward_z(3)
+    forward_y(1)
+    forward_y(3)
+    forward_q(1)
+    forward_z(2)
+    forward_y(2)
 
     acc[...] = jnp.zeros_like(acc)
     dqt[...] = jnp.zeros_like(dqt)
@@ -239,19 +295,34 @@
 
     def send_y(c):
         for n in range(1, SIDE):
-            part[c, n - 1] = acc[SIDE * c + n].astype(BF16)
-            ry_go[c][n - 1].start()
+            part[c, n - 1, 0:192] = acc[SIDE * c + n, 0:192].astype(BF16)
+            ry_most[c][n - 1].start()
+        if c:
+            lpart[c - 1] = acc[SIDE * c : SIDE * (c + 1), 192:256].astype(BF16)
+            rz_last[c].start()
 
     def sum_y(c):
-        arrive(ry_go[c])
-        total = acc[SIDE * c]
+        arrive(ry_most[c])
+        total = acc[SIDE * c, 0:192]
         for n in range(SIDE - 1):
-            total = total + ybuf[c, n].astype(F32)
+            total = total + ybuf[c, n, 0:192].astype(F32)
         return total
 
     def send_z(c):
         zpart[c - 1] = sum_y(c).astype(BF16)
-        rz_go[c].start()
+        rz_most[c].start()
+
+    def turn_last():
+        arrive(rz_last[1:])
+        for n in (2, 1, 3, 0):
+            total = acc[n, 192:256]
+            for s in range(SIDE - 1):
+                total = total + lbuf[s, n].astype(F32)
+            if n:
+                part[0, n - 1, 192:256] = total.astype(BF16)
+                ry_last[n - 1].start()
+            else:
+                acc[0, 192:256] = total
 
     def send_x(d):
         xpart[d - 1] = dqt[d].astype(BF16)
@@ -273,23 +344,34 @@
         out[ROWS : 2 * ROWS, :] = total[128:256].T.astype(BF16)
 
     def finish_kv():
-        own = sum_y(0)
-        arrive(rz_go[1:])
+        most_sum = sum_y(0)
+        arrive(rz_most[1:])
         for n in range(SIDE - 1):
-            own = own + zbuf[n].astype(F32)
-        out[512:640, :] = (own[0:128] * SCALE).astype(BF16)
-        out[640:768, :] = own[128:256].astype(BF16)
+            most_sum = most_sum + zbuf[n].astype(F32)
+        out[512:640, :] = (most_sum[0:128] * SCALE).astype(BF16)
+        out[640:704, :] = most_sum[128:192].astype(BF16)
+        arrive(ry_last)
+        last_sum = acc[0, 192:256]
+        for n in range(SIDE - 1):
+            last_sum = last_sum + ybuf[0, n, 192:256].astype(F32)
+        out[704:768, :] = last_sum.astype(BF16)
+
+    def need_y(c):
+        arrive(y_head[c])
+        if c:
+            arrive([z_tail[n][c - 1] for n in range(SIDE)])
 
     def need_q(d):
-        arrive(q_go[d] + [meta_go[d]])
+        arrive(q_come[d] + [meta_go[d]])
         turn(d)
 
     actions = {
-        "need_y": lambda c: arrive(y_go[c]),
+        "need_y": need_y,
         "need_q": need_q,
         "send_y": send_y,
         "send_z": send_z,
         "send_x": send_x,
+        "turn_last": lambda unused: turn_last(),
     }
 
     def act(names):
@@ -308,7 +390,7 @@
         return carry
 
     turn(0)
-    arrive(y_go[0])
+    need_y(0)
     own_early()
     lax.fori_loop(0, len(ORDER), loop_step, 0)
     act(LAST)
@@ -318,12 +400,12 @@
         copy.wait_send()
 
 
-COPIES = 9 + 3 + 12 + 12 + 3 + 3
+COPIES = 3 + 12 + 3 + 12 + 8 + 4 + 3 + 12 + 3 + 3 + 3 + 3
 GROUPS = {"t": (0, 1, 3), "s": (2,)}
 ORDER = (("t", 0), ("t", 1), ("t", 3), ("s", 1), ("s", 3), ("t", 2), ("s", 2), ("s", 0))
 BEFORE = {0: ("need_q1", "need_q3"), 1: ("need_y1",), 2: ("need_y3",), 3: ("need_q2",), 5: ("need_y2",)}
 AFTER = {3: ("send_y1",), 4: ("send_y3",), 5: ("send_x1", "send_x3"), 6: ("send_y2", "send_z1")}
-LAST = ("send_x2", "send_y0", "send_z3", "send_z2")
+LAST = ("send_x2", "send_y0", "send_z3", "turn_last0", "send_z2")
 
 
 def body(queries, keys, values, grad_out, saved_stats, positions):
@@ -345,8 +427,10 @@
             pltpu.VMEM((4, 256, ROWS), F32),
             pltpu.VMEM((4, 3, 256, DIM), BF16),
             pltpu.VMEM((4, 3, 256, DIM), BF16),
-            pltpu.VMEM((3, 256, DIM), BF16),
-            pltpu.VMEM((3, 256, DIM), BF16),
+            pltpu.VMEM((3, 192, DIM), BF16),
+            pltpu.VMEM((3, 192, DIM), BF16),
+            pltpu.VMEM((3, 4, 64, DIM), BF16),
+            pltpu.VMEM((3, 4, 64, DIM), BF16),
             pltpu.VMEM((3, 256, ROWS), BF16),
             pltpu.VMEM((3, 256, ROWS), BF16),
             pltpu.SemaphoreType.DMA((7,)),

time: 42.5 us -> 40.1 us (0.944)
  the two profiles are of different devices: /device:TPU:128 before, /device:TPU:134 now
where the time goes in v3:
time: 40.1 us; the launch traced here: 39.9 us
  Pallas kernels  36.3 us (91%)
  local copies, waits for them, and re-layouts  2.97 us (7%)
  between operations  0.64 us (2%)
    pallas_call x1, Pallas kernels, body(): pl.pallas_call(kernel, out_shape=jax.ShapeDtypeStruct((768, DIM), BF16),...  36.3 us
    slice x1, local copies, waits for them, and re-layouts, body(): grads[0:512].reshape(128, GROUP, DIM)  1.57 us
    reshape x1, local copies, waits for them, and re-layouts, body(): grads[640:768].reshape(128, 1, DIM)  1.4 us

profile of v3, /device:TPU:134, one launch (start us, length us, event | category | flops | bytes accessed | tf_op | source)
XLA Modules:
  0.0 39.9 jit_solution(5143351520358456940)
XLA Ops:
  0.6 36.3 %shard_map.85 = bf16[768,128]{1,0:T(8,128)(2,1)} custom-call(bf16[512,128]{1,0:T(8,128)(2,1)} %bitcast.11, bf16[128,128]{1,0:T(8,128)(2,1)} %bitcast.14, bf16[128,128]{1,0:T(8,128)(2,1)} %bitcast.15, bf16[512,128]{1,0:T(8,128)(2,1)} %bitcast.12, f32[8,128]{1,0:T(8,128)} %bitcast.16, s32[1,128]{1,0:T(1,128)} %bitcast.17), custom_call_target="tpu_custom_call" | custom-call | tf_op jit(solution)/shard_map/pallas_call | solution.py:414
  36.9 1.4 %slice_bitcast_fusion = (bf16[128,1,128]{2,0,1:T(8,128)(2,1)}, bf16[128,1,128]{2,0,1:T(8,128)(2,1)}) fusion(bf16[768,128]{1,0:T(8,128)(2,1)} %shard_map.85), kind=kLoop, calls=%fused_computation | loop fusion | bytes 131072 | tf_op jit(solution)/shard_map/reshape | solution.py:454
  38.3 1.6 %slice.9 = bf16[512,128]{1,0:T(8,128)(2,1)} slice(bf16[768,128]{1,0:T(8,128)(2,1)} %shard_map.85), slice={[0:512], [0:128]} | slice | bytes 262144 | tf_op jit(solution)/shard_map/slice | solution.py:452

commit v4 on v3

--- a/solution.py
+++ b/solution.py
@@ -154,15 +154,18 @@
         for copy in copies:
             copy.start()
 
+    def sent(copies):
+        for copy in copies:
+            copy.wait_send()
+
     def arrive(copies):
         for copy in copies:
             copy.wait_recv()
 
     pl.semaphore_wait(barrier, len(peers))
-    start((z_head[1], z_head[3], z_head[2]))
+    start((z_head[1], z_head[3]))
     start(y_tail[1:])
     start(y_head[0])
-    start(z_tail[0])
     for load in loads[0:2]:
         load.wait()
     for h in range(2):
@@ -201,13 +204,15 @@
         start(z_tail[n])
 
     forward_z(1)
-    forward_q(0)
+    start([z_head[2]])
     forward_z(3)
+    start(z_tail[0])
     forward_y(1)
     forward_y(3)
+    forward_y(2)
+    forward_z(2)
+    forward_q(0)
     forward_q(1)
-    forward_z(2)
-    forward_y(2)
 
     acc[...] = jnp.zeros_like(acc)
     dqt[...] = jnp.zeros_like(dqt)
@@ -294,12 +299,12 @@
             acc[slots, SPAN * n : SPAN * (n + 1), :] += tot[n].reshape(SIDE, SPAN, DIM)
 
     def send_y(c):
-        for n in range(1, SIDE):
-            part[c, n - 1, 0:192] = acc[SIDE * c + n, 0:192].astype(BF16)
-            ry_most[c][n - 1].start()
         if c:
             lpart[c - 1] = acc[SIDE * c : SIDE * (c + 1), 192:256].astype(BF16)
             rz_last[c].start()
+        for n in (2, 1, 3):
+            part[c, n - 1, 0:192] = acc[SIDE * c + n, 0:192].astype(BF16)
+            ry_most[c][n - 1].start()
 
     def sum_y(c):
         arrive(ry_most[c])
@@ -371,7 +376,6 @@
         "send_y": send_y,
         "send_z": send_z,
         "send_x": send_x,
-        "turn_last": lambda unused: turn_last(),
     }
 
     def act(names):
@@ -394,18 +398,23 @@
     own_early()
     lax.fori_loop(0, len(ORDER), loop_step, 0)
     act(LAST)
+    sent(links.made[:45])
+    turn_last()
+    sent(ry_most[1] + ry_most[3] + rz_last[1:] + rx_go[1:2] + rx_go[3:4] + [rz_most[1], rz_most[3]])
+    send_z(2)
+    sent(ry_most[2] + ry_most[0] + [rx_go[2]])
     finish_x()
+    sent(ry_last)
     finish_kv()
-    for copy in links.made:
-        copy.wait_send()
+    sent([rz_most[2]])
 
 
 COPIES = 3 + 12 + 3 + 12 + 8 + 4 + 3 + 12 + 3 + 3 + 3 + 3
-GROUPS = {"t": (0, 1, 3), "s": (2,)}
-ORDER = (("t", 0), ("t", 1), ("t", 3), ("s", 1), ("s", 3), ("t", 2), ("s", 2), ("s", 0))
+GROUPS = {"t": (0, 1, 3), "s": (2,), "q": (0, 1, 2, 3)}
+ORDER = (("t", 0), ("t", 1), ("t", 3), ("s", 1), ("s", 3), ("q", 2), ("s", 0))
 BEFORE = {0: ("need_q1", "need_q3"), 1: ("need_y1",), 2: ("need_y3",), 3: ("need_q2",), 5: ("need_y2",)}
-AFTER = {3: ("send_y1",), 4: ("send_y3",), 5: ("send_x1", "send_x3"), 6: ("send_y2", "send_z1")}
-LAST = ("send_x2", "send_y0", "send_z3", "turn_last0", "send_z2")
+AFTER = {3: ("send_y1",), 4: ("send_y3",), 5: ("send_y2", "send_x1", "send_x3", "send_z1")}
+LAST = ("send_x2", "send_y0", "send_z3")
 
 
 def body(queries, keys, values, grad_out, saved_stats, positions):

time: 40.1 us -> 40 us (level)
  the two profiles are of different devices: /device:TPU:134 before, /device:TPU:192 now
where the time goes in v4:
time: 40 us; the launch traced here: 39.8 us
  Pallas kernels  36.2 us (91%)
  local copies, waits for them, and re-layouts  2.97 us (7%)
  between operations  0.64 us (2%)
    pallas_call x1, Pallas kernels, body(): pl.pallas_call(kernel, out_shape=jax.ShapeDtypeStruct((768, DIM), BF16),...  36.2 us
    slice x1, local copies, waits for them, and re-layouts, body(): grads[0:512].reshape(128, GROUP, DIM)  1.57 us
    reshape x1, local copies, waits for them, and re-layouts, body(): grads[640:768].reshape(128, 1, DIM)  1.4 us

profile of v4, /device:TPU:192, one launch (start us, length us, event | category | flops | bytes accessed | tf_op | source)
XLA Modules:
  0.0 39.8 jit_solution(17261710331652477668)
XLA Ops:
  0.6 36.2 %shard_map.85 = bf16[768,128]{1,0:T(8,128)(2,1)} custom-call(bf16[512,128]{1,0:T(8,128)(2,1)} %bitcast.11, bf16[128,128]{1,0:T(8,128)(2,1)} %bitcast.14, bf16[128,128]{1,0:T(8,128)(2,1)} %bitcast.15, bf16[512,128]{1,0:T(8,128)(2,1)} %bitcast.12, f32[8,128]{1,0:T(8,128)} %bitcast.16, s32[1,128]{1,0:T(1,128)} %bitcast.17), custom_call_target="tpu_custom_call" | custom-call | tf_op jit(solution)/shard_map/pallas_call | solution.py:423
  36.8 1.4 %slice_bitcast_fusion = (bf16[128,1,128]{2,0,1:T(8,128)(2,1)}, bf16[128,1,128]{2,0,1:T(8,128)(2,1)}) fusion(bf16[768,128]{1,0:T(8,128)(2,1)} %shard_map.85), kind=kLoop, calls=%fused_computation | loop fusion | bytes 131072 | tf_op jit(solution)/shard_map/reshape | solution.py:463
  38.2 1.6 %slice.9 = bf16[512,128]{1,0:T(8,128)(2,1)} slice(bf16[768,128]{1,0:T(8,128)(2,1)} %shard_map.85), slice={[0:512], [0:128]} | slice | bytes 262144 | tf_op jit(solution)/shard_map/slice | solution.py:461

commit v5 on v4

--- a/solution.py
+++ b/solution.py
@@ -413,8 +413,8 @@
 GROUPS = {"t": (0, 1, 3), "s": (2,), "q": (0, 1, 2, 3)}
 ORDER = (("t", 0), ("t", 1), ("t", 3), ("s", 1), ("s", 3), ("q", 2), ("s", 0))
 BEFORE = {0: ("need_q1", "need_q3"), 1: ("need_y1",), 2: ("need_y3",), 3: ("need_q2",), 5: ("need_y2",)}
-AFTER = {3: ("send_y1",), 4: ("send_y3",), 5: ("send_y2", "send_x1", "send_x3", "send_z1")}
-LAST = ("send_x2", "send_y0", "send_z3")
+AFTER = {3: ("send_y1",), 4: ("send_y3",), 5: ("send_y2", "send_x1", "send_x3")}
+LAST = ("send_y0", "send_x2", "send_z1", "send_z3")
 
 
 def body(queries, keys, values, grad_out, saved_stats, positions):

time: 40 us -> 40 us (level)
  no operation moved by 1% of the time
where the time goes in v5:
time: 40 us; the launch traced here: 39.8 us
  Pallas kernels  36.2 us (91%)
  local copies, waits for them, and re-layouts  2.97 us (7%)
  between operations  0.64 us (2%)
    pallas_call x1, Pallas kernels, body(): pl.pallas_call(kernel, out_shape=jax.ShapeDtypeStruct((768, DIM), BF16),...  36.2 us
    slice x1, local copies, waits for them, and re-layouts, body(): grads[0:512].reshape(128, GROUP, DIM)  1.57 us
    reshape x1, local copies, waits for them, and re-layouts, body(): grads[640:768].reshape(128, 1, DIM)  1.4 us

profile of v5, /device:TPU:192, one launch (start us, length us, event | category | flops | bytes accessed | tf_op | source)
XLA Modules:
  0.0 39.8 jit_solution(10633690896357381236)
XLA Ops:
  0.6 36.2 %shard_map.85 = bf16[768,128]{1,0:T(8,128)(2,1)} custom-call(bf16[512,128]{1,0:T(8,128)(2,1)} %bitcast.11, bf16[128,128]{1,0:T(8,128)(2,1)} %bitcast.14, bf16[128,128]{1,0:T(8,128)(2,1)} %bitcast.15, bf16[512,128]{1,0:T(8,128)(2,1)} %bitcast.12, f32[8,128]{1,0:T(8,128)} %bitcast.16, s32[1,128]{1,0:T(1,128)} %bitcast.17), custom_call_target="tpu_custom_call" | custom-call | tf_op jit(solution)/shard_map/pallas_call | solution.py:423
  36.8 1.4 %slice_bitcast_fusion = (bf16[128,1,128]{2,0,1:T(8,128)(2,1)}, bf16[128,1,128]{2,0,1:T(8,128)(2,1)}) fusion(bf16[768,128]{1,0:T(8,128)(2,1)} %shard_map.85), kind=kLoop, calls=%fused_computation | loop fusion | bytes 131072 | tf_op jit(solution)/shard_map/reshape | solution.py:463
  38.2 1.6 %slice.9 = bf16[512,128]{1,0:T(8,128)(2,1)} slice(bf16[768,128]{1,0:T(8,128)(2,1)} %shard_map.85), slice={[0:512], [0:128]} | slice | bytes 262144 | tf_op jit(solution)/shard_map/slice | solution.py:461

commit v6 on v4

--- a/solution.py
+++ b/solution.py
@@ -411,9 +411,9 @@
 
 COPIES = 3 + 12 + 3 + 12 + 8 + 4 + 3 + 12 + 3 + 3 + 3 + 3
 GROUPS = {"t": (0, 1, 3), "s": (2,), "q": (0, 1, 2, 3)}
-ORDER = (("t", 0), ("t", 1), ("t", 3), ("s", 1), ("s", 3), ("q", 2), ("s", 0))
-BEFORE = {0: ("need_q1", "need_q3"), 1: ("need_y1",), 2: ("need_y3",), 3: ("need_q2",), 5: ("need_y2",)}
-AFTER = {3: ("send_y1",), 4: ("send_y3",), 5: ("send_y2", "send_x1", "send_x3", "send_z1")}
+ORDER = (("t", 0), ("t", 1), ("s", 1), ("t", 3), ("s", 3), ("q", 2), ("s", 0))
+BEFORE = {0: ("need_q1", "need_q3"), 1: ("need_y1",), 2: ("need_q2",), 3: ("need_y3",), 5: ("need_y2",)}
+AFTER = {2: ("send_y1",), 4: ("send_y3",), 5: ("send_y2", "send_x1", "send_x3", "send_z1")}
 LAST = ("send_x2", "send_y0", "send_z3")
 
 

time: 40 us -> 40.5 us (1.012)
  the two profiles are of different devices: /device:TPU:192 before, /device:TPU:128 now
where the time goes in v6:
time: 40.5 us; the launch traced here: 40.3 us
  Pallas kernels  36.7 us (91%)
  local copies, waits for them, and re-layouts  2.97 us (7%)
  between operations  0.64 us (2%)
    pallas_call x1, Pallas kernels, body(): pl.pallas_call(kernel, out_shape=jax.ShapeDtypeStruct((768, DIM), BF16),...  36.7 us
    slice x1, local copies, waits for them, and re-layouts, body(): grads[0:512].reshape(128, GROUP, DIM)  1.57 us
    reshape x1, local copies, waits for them, and re-layouts, body(): grads[640:768].reshape(128, 1, DIM)  1.4 us

profile of v6, /device:TPU:128, one launch (start us, length us, event | category | flops | bytes accessed | tf_op | source)
XLA Modules:
  0.0 40.3 jit_solution(15509673219697540152)
XLA Ops:
  0.6 36.7 %shard_map.85 = bf16[768,128]{1,0:T(8,128)(2,1)} custom-call(bf16[512,128]{1,0:T(8,128)(2,1)} %bitcast.11, bf16[128,128]{1,0:T(8,128)(2,1)} %bitcast.14, bf16[128,128]{1,0:T(8,128)(2,1)} %bitcast.15, bf16[512,128]{1,0:T(8,128)(2,1)} %bitcast.12, f32[8,128]{1,0:T(8,128)} %bitcast.16, s32[1,128]{1,0:T(1,128)} %bitcast.17), custom_call_target="tpu_custom_call" | custom-call | tf_op jit(solution)/shard_map/pallas_call | solution.py:423
  37.3 1.4 %slice_bitcast_fusion = (bf16[128,1,128]{2,0,1:T(8,128)(2,1)}, bf16[128,1,128]{2,0,1:T(8,128)(2,1)}) fusion(bf16[768,128]{1,0:T(8,128)(2,1)} %shard_map.85), kind=kLoop, calls=%fused_computation | loop fusion | bytes 131072 | tf_op jit(solution)/shard_map/reshape | solution.py:463
  38.7 1.6 %slice.9 = bf16[512,128]{1,0:T(8,128)(2,1)} slice(bf16[768,128]{1,0:T(8,128)(2,1)} %shard_map.85), slice={[0:512], [0:128]} | slice | bytes 262144 | tf_op jit(solution)/shard_map/slice | solution.py:461
